TPU v7x, 128 devices: a whole 4x4x4 slice. The times are simulated.
128 devices in a mesh: frames: 64 (over z, x_lo, y, core), bands: 2 (over x_hi).
Axes of the slice: x: 4 (x_hi: 2, x_lo: 2; x = x_hi * 2 + x_lo), y: 4, z: 4, core: 2. Of those that a mesh axis runs over, the one named last changes fastest.
Arguments:
- spectrum: bfloat16 [1, 4096, 1280], P(None, 'frames'), may hold values from -6 to 6
- band_widths: int32 [32], replicated, may hold values from 1 to 64, 640 in all
- band_weight: bfloat16 [32, 128, 384], P('bands'), may hold values from -0.5 to 0.5
- qkv_time: bfloat16 [384, 768], replicated
- out_time: bfloat16 [256, 384], replicated, may hold values from -0.375 to 0.375
- qkv_band: bfloat16 [384, 768], replicated
- out_band: bfloat16 [256, 384], replicated, may hold values from -0.375 to 0.375
- cotangent: bfloat16 [1, 32, 4096, 384], P(None, 'bands', 'frames'), may hold values from -0.059814453 to 0.059814453
Outputs:
- latent: bfloat16 [1, 32, 4096, 384], P(None, 'bands', 'frames')
- band_grad: float32 [32, 128, 384], P('bands')
- weight_grads: float32 [786432], P(('frames', 'bands'))
Inputs may be any that keep to these rules, and one draw needn't show every extreme that they name: `band_widths`: the 32 band widths sum to 640 and one of them equals 64.
All inputs are finite; a program needn't handle non-finite values.
Results may differ from a plain program's by a relative error of at most 0.022.
Values may be sent and summed in bfloat16 or wider, within the bound.
A program may use at most 192 MiB of HBM per device.

v0:
```python
import math

import jax
import jax.numpy as jnp
from jax import lax
from jax.sharding import PartitionSpec as P

H = 4


EPS = 1e-05
THETA = 10000.0


def rms_norm(values):
    return values * lax.rsqrt(jnp.mean(values * values, axis=-1, keepdims=True) + EPS)


def lift(rounded):
    return lax.optimization_barrier(rounded).astype(jnp.float32)


def rotary_angles(positions, head_size):
    exponent = jnp.arange(head_size // 2, dtype=jnp.int32).astype(jnp.float32)
    frequency = jnp.exp(exponent * (-2.0 * math.log(THETA) / head_size))
    return positions.astype(jnp.float32)[:, None] * frequency[None, :]


def rotate(vectors, angles):
    half_size = vectors.shape[-1] // 2
    leading = vectors[..., :half_size]
    trailing = vectors[..., half_size:]
    cosine = jnp.cos(angles)
    sine_part = jnp.sin(angles)
    return jnp.concatenate(
        [leading * cosine - trailing * sine_part, leading * sine_part + trailing * cosine], axis=-1
    )


def split_heads(values, n_heads):
    return values.reshape(values.shape[:-1] + (n_heads, values.shape[-1] // n_heads))


def merge_heads(values):
    return values.reshape(values.shape[:-2] + (values.shape[-2] * values.shape[-1],))


def band_features(spectrum, widths, first_band, band_count, feature_span):
    band_ends = jnp.cumsum(widths)
    starts = band_ends - widths
    own_starts = lax.dynamic_slice_in_dim(starts, first_band, band_count)
    own_widths = lax.dynamic_slice_in_dim(widths, first_band, band_count)
    offsets = jnp.arange(feature_span, dtype=jnp.int32)
    columns = (2 * own_starts[:, None] + offsets[None, :]).reshape(-1)
    padded = jnp.pad(spectrum, ((0, 0), (0, 0), (0, feature_span)))
    picked = jnp.take(padded, columns, axis=2)
    picked = picked.reshape(spectrum.shape[0], spectrum.shape[1], band_count, feature_span)
    keep_mask = offsets[None, :] < 2 * own_widths[:, None]
    return jnp.where(keep_mask, picked, jnp.zeros((), picked.dtype))


def project_bands(features, matrix):
    return jnp.einsum("btkj,kjd->bktd", features.astype(jnp.float32), matrix).astype(jnp.bfloat16)


def qkv_rotated(residual, matrix, angles, n_heads):
    inner_width = matrix.shape[1] // 3
    normed = rms_norm(residual).astype(jnp.bfloat16)
    projected = jnp.dot(lift(normed), matrix)
    query_part = rotate(split_heads(projected[..., :inner_width], n_heads), angles)
    key_part = rotate(split_heads(projected[..., inner_width : 2 * inner_width], n_heads), angles)
    value_part = split_heads(projected[..., 2 * inner_width :], n_heads)
    return (
        query_part.astype(jnp.bfloat16),
        key_part.astype(jnp.bfloat16),
        value_part.astype(jnp.bfloat16),
    )


def block_weights(q_block, keys_f):
    factor = q_block.shape[-1] ** (-0.5)
    scores = jnp.einsum("ntd,nsd->nts", lift(q_block), keys_f) * factor
    return jax.nn.softmax(scores, axis=-1).astype(jnp.bfloat16)


def attention_items(queries, keys_f, values_f):
    n_items, n_time, head_size = queries.shape
    block = math.gcd(512, n_time)
    saved_weights = jax.checkpoint(block_weights)

    def one_block(q_block):
        probs = lift(saved_weights(q_block, keys_f))
        return jnp.einsum("nts,nsd->ntd", probs, values_f).astype(jnp.bfloat16)

    blocks = queries.reshape(n_items, n_time // block, block, head_size).transpose(1, 0, 2, 3)
    result = lax.map(one_block, blocks)
    return result.transpose(1, 0, 2, 3).reshape(n_items, n_time, head_size)


def band_core(queries, keys_f, values_f, n_heads):
    head_size = queries.shape[-1] // n_heads
    q_heads = split_heads(lift(queries), n_heads)
    k_heads = split_heads(keys_f, n_heads)
    v_heads = split_heads(values_f, n_heads)
    scores = jnp.einsum("bqthd,bkthd->bthqk", q_heads, k_heads) * head_size ** (-0.5)
    probs = lift(jax.nn.softmax(scores, axis=-1).astype(jnp.bfloat16))
    attended = jnp.einsum("bthqk,bkthd->bqthd", probs, v_heads).astype(jnp.bfloat16)
    return attended.reshape(queries.shape)


def residual_out(residual, attended, out_matrix):
    return (residual + jnp.dot(lift(attended), out_matrix)).astype(jnp.bfloat16)


def to_items(tensor):
    n_batch, n_bands, n_rows, n_heads, head_size = tensor.shape
    return tensor.transpose(0, 1, 3, 2, 4).reshape(n_batch * n_bands * n_heads, n_rows * head_size)


def from_items(tensor, n_batch, n_bands, n_heads, head_size):
    n_rows = tensor.shape[1] // head_size
    shaped = tensor.reshape(n_batch, n_bands, n_heads, n_rows, head_size)
    return shaped.transpose(0, 1, 3, 2, 4).reshape(n_batch, n_bands, n_rows, n_heads * head_size)


def shards(spectrum, band_widths, band_weight, qkv_time, out_time, qkv_band, out_band, cotangent):
    n_batch = spectrum.shape[0]
    frames_dev = spectrum.shape[1]
    bands_dev = band_weight.shape[0]
    n_heads = H
    head_size = out_time.shape[0] // n_heads
    first_band = lax.axis_index("bands") * bands_dev
    first_frame = lax.axis_index("frames") * frames_dev
    w_band = band_weight.astype(jnp.float32)
    w_qkv_t = qkv_time.astype(jnp.float32)
    w_out_t = out_time.astype(jnp.float32)
    w_qkv_b = qkv_band.astype(jnp.float32)
    w_out_b = out_band.astype(jnp.float32)
    features = band_features(spectrum, band_widths, first_band, bands_dev, band_weight.shape[1])
    latent_in, pull_split = jax.vjp(lambda matrix: project_bands(features, matrix), w_band)
    residual = lift(latent_in)
    frame_angles = rotary_angles(first_frame + jnp.arange(frames_dev, dtype=jnp.int32), head_size)

    def time_pre(resid, matrix):
        rotated = qkv_rotated(resid, matrix, frame_angles[:, None, :], n_heads)
        return (to_items(rotated[0]), to_items(rotated[1]), to_items(rotated[2]))

    (t_query, t_key, t_value), pull_tpre = jax.vjp(time_pre, residual, w_qkv_t)
    seq_query, seq_key, seq_value = (
        lax.all_to_all(t_query, "frames", split_axis=0, concat_axis=1, tiled=True),
        lax.all_to_all(t_key, "frames", split_axis=0, concat_axis=1, tiled=True),
        lax.all_to_all(t_value, "frames", split_axis=0, concat_axis=1, tiled=True),
    )

    def time_core(q_seq, k_seq, v_seq):
        n_items = q_seq.shape[0]
        keys_f = lift(k_seq.reshape(n_items, -1, head_size))
        values_f = lift(v_seq.reshape(n_items, -1, head_size))
        result = attention_items(q_seq.reshape(n_items, -1, head_size), keys_f, values_f)
        return result.reshape(n_items, -1)

    seq_out, pull_core = jax.vjp(time_core, seq_query, seq_key, seq_value)
    own_out = lax.all_to_all(seq_out, "frames", split_axis=1, concat_axis=0, tiled=True)

    def time_tail(resid, attended_items, out_matrix):
        attended = from_items(attended_items, n_batch, bands_dev, n_heads, head_size)
        return residual_out(resid, attended, out_matrix)

    second, pull_tpost = jax.vjp(time_tail, residual, own_out, w_out_t)
    second_f = lift(second)
    band_angles = rotary_angles(first_band + jnp.arange(bands_dev, dtype=jnp.int32), head_size)

    def band_pre(resid, matrix):
        rotated = qkv_rotated(resid, matrix, band_angles[:, None, None, :], n_heads)
        return (merge_heads(rotated[0]), merge_heads(rotated[1]), merge_heads(rotated[2]))

    (b_query, b_key, b_value), pull_bpre = jax.vjp(band_pre, second_f, w_qkv_b)
    all_key, all_value = (
        lax.all_gather(b_key, "bands", axis=1, tiled=True),
        lax.all_gather(b_value, "bands", axis=1, tiled=True),
    )
    keys_f = lift(all_key)
    values_f = lift(all_value)

    def band_full(resid, queries, key_rows, value_rows, out_matrix):
        return residual_out(resid, band_core(queries, key_rows, value_rows, n_heads), out_matrix)

    latent, pull_bpost = jax.vjp(band_full, second_f, b_query, keys_f, values_f, w_out_b)
    d_second_a, d_query, d_keys_f, d_values_f, g_out_b = pull_bpost(cotangent)
    sum_key, sum_value = (
        lax.psum_scatter(
            d_keys_f.astype(jnp.bfloat16), "bands", scatter_dimension=1, tiled=True
        ).astype(jnp.float32),
        lax.psum_scatter(
            d_values_f.astype(jnp.bfloat16), "bands", scatter_dimension=1, tiled=True
        ).astype(jnp.float32),
    )
    d_second_b, g_qkv_b = pull_bpre(
        (d_query, sum_key.astype(jnp.bfloat16), sum_value.astype(jnp.bfloat16))
    )
    d_second = (d_second_a + d_second_b).astype(jnp.bfloat16)
    d_resid_a, d_own_out, g_out_t = pull_tpost(d_second)
    d_seq_out = lax.all_to_all(d_own_out, "frames", split_axis=0, concat_axis=1, tiled=True)
    d_seq_query, d_seq_key, d_seq_value = pull_core(d_seq_out)
    back_time = (
        lax.all_to_all(d_seq_query, "frames", split_axis=1, concat_axis=0, tiled=True),
        lax.all_to_all(d_seq_key, "frames", split_axis=1, concat_axis=0, tiled=True),
        lax.all_to_all(d_seq_value, "frames", split_axis=1, concat_axis=0, tiled=True),
    )
    d_resid_b, g_qkv_t = pull_tpre((back_time[0], back_time[1], back_time[2]))
    d_latent_in = (d_resid_a + d_resid_b).astype(jnp.bfloat16)
    (g_band,) = pull_split(d_latent_in)
    band_grad = lax.psum(g_band, "frames")
    flat = jnp.concatenate(
        [grad_part.reshape(-1) for grad_part in (g_qkv_t, g_out_t, g_qkv_b, g_out_b)]
    )
    own_share = lax.psum_scatter(flat, ("frames", "bands"), scatter_dimension=0, tiled=True)
    return (latent, band_grad, own_share)


def solution(mesh):
    placed = (
        P(None, "frames", None),
        P(),
        P("bands", None, None),
        P(),
        P(),
        P(),
        P(),
        P(None, "bands", "frames", None),
    )
    return jax.shard_map(
        shards,
        mesh=mesh,
        in_specs=placed,
        out_specs=(
            P(None, "bands", "frames", None),
            P("bands", None, None),
            P(("frames", "bands")),
        ),
        check_vma=False,
    )
```

profile of v0, /device:TPU:1, one launch (start us, length us, event | category | flops | bytes accessed | tf_op | source)
XLA Modules:
  0.0 1498.3 jit_solution(4452169934434598850)
XLA Ops:
  11.0 6.2 gather_fusion
  25.0 5.5 fusion.198
  32.6 5.4 fusion.199
  56.4 10.9 all-to-all-start.1
  79.9 7.3 all-to-all-start
  99.3 5.2 all-to-all-start.2
  127.5 82.4 %while.31 = (s32[]{:T(128)}, bf16[8,1,512,64]{2,3,1,0:T(8,128)(2,1)}, bf16[8,1,512,4096]{3,2,1,0:T(8,128)(2,1)}, bf16[8,1,512,64]{3,2,1,0:T(8,128)(2,1)}, bf16[1...) while((s32[]{:T(128)}, bf16[8,1,512,64]{2,3,1,0:T(8,128)(2,1)}, ...), condition=%wide.region_5.6_spmd, body=%wide.region_2.5_spmd.sunk | while | flops 557841408 | bytes 47459408 | solution.py:96
  222.9 9.0 all-to-all-start.3
  232.1 12.3 all-to-all-done.3
  271.0 7.7 subtract_convert_fusion.1
  296.5 10.5 all-gather.5.cloned.1.call-done
  311.4 5.9 fusion.200
  317.4 16.0 %all-gather.3.cloned.1.call-done = bf16[1,32,64,256]{3,2,0,1:T(8,128)(2,1)} async-done(((bf16[1,16,64,256]{3,2,0,1:T(8,128)(2,1)}), bf16[1,32,64,256]{3,2,0,1:T(8,128)(2,1)}) %all-gather.3.cloned.1.call-update) | async-done | bytes 1048592 | tf_op jit(solution)/shard_map/all_gather | solution.py:180
  380.8 7.8 multiply_add_fusion.7
  424.6 8.4 all-to-all-start.4
  433.0 12.3 all-to-all-done.4
  453.5 187.9 %while.32 = (s32[]{:T(128)}, f32[1,4096,64]{1,2,0:T(8,128)}, f32[1,4096,64]{1,2,0:T(8,128)}, bf16[8,1,512,64]{2,3,1,0:T(8,128)(2,1)S(1)}, bf16[8,1,512,64]{3,2,1...) while((s32[]{:T(128)}, f32[1,4096,64]{1,2,0:T(8,128)}, ...), condition=%wide.region_17.18_spmd.clone, body=%wide.region_13.17_spmd.clone.sunk | while | flops 1383071744 | bytes 86208184 | solution.py:96
  672.4 9.4 all-to-all-start.7
  701.6 5.3 convert_reduce_fusion.1
  710.0 8.8 all-to-all-start.5
  723.6 5.3 convert_reduce_fusion
  731.9 6.8 multiply_add_fusion.3
  786.1 144.3 %all-reduce.21.cloned.1.call-done = f32[786432]{0:T(1024)} async-done(((f32[786432]{0:T(1024)}), f32[786432]{0:T(1024)}) %all-reduce.21.cloned.1.call-update) | async-done | bytes 3145744
  931.9 555.3 %all-reduce.19.cloned.1.call-done = f32[16,128,384]{2,1,0:T(8,128)} async-done(((f32[16,128,384]{2,1,0:T(8,128)}), f32[16,128,384]{2,1,0:T(8,128)}) %all-reduce.19.cloned.1.call-update) | async-done | bytes 3145744 | tf_op jit(solution)/shard_map/psum | solution.py:213
  (447 shorter events, 616.7 us)
Async XLA Ops:
  7.2 10.4 copy-start
  9.8 7.8 copy-start.47
  18.1 239.8 %copy-start.3 = (bf16[1,16,64,384]{3,2,1,0:T(8,128)(2,1)}, bf16[1,16,64,384]{3,2,1,0:T(8,128)(2,1)S(1)}, u32[]{:S(2)}) copy-start(bf16[1,16,64,384]{3,2,1,0:T(8,128)(2,1)S(1)} %fusion.136) | copy-start | bytes 2359300
  56.4 23.4 %all-to-all-start.1 = ((bf16[64,2,2048]{2,1,0:T(2,128)(2,1)}), bf16[64,2,2048]{2,1,0:T(2,128)(2,1)S(1)}, u32[]{:S(2)}, u32[]{:S(2)}) async-start(bf16[64,2,2048]{2,1,0:T(2,128)(2,1)} %reshape.1010), calls=%async_computation.1 | async-start | bytes 1048576 | tf_op jit(solution)/shard_map/all_to_all | solution.py:151
  79.9 19.5 %all-to-all-start = ((bf16[64,2,2048]{2,1,0:T(2,128)(2,1)}), bf16[64,2,2048]{2,1,0:T(2,128)(2,1)}, u32[]{:S(2)}, u32[]{:S(2)}) async-start(bf16[64,2,2048]{2,1,0:T(2,128)(2,1)} %reshape.1008), calls=%async_computation | async-start | bytes 1048576 | tf_op jit(solution)/shard_map/all_to_all | solution.py:150
  99.3 19.0 %all-to-all-start.2 = ((bf16[64,2,2048]{2,1,0:T(2,128)(2,1)}), bf16[64,2,2048]{2,1,0:T(2,128)(2,1)}, u32[]{:S(2)}, u32[]{:S(2)}) async-start(bf16[64,2,2048]{2,1,0:T(2,128)(2,1)} %reshape.1012), calls=%async_computation.2 | async-start | bytes 1048576 | tf_op jit(solution)/shard_map/all_to_all | solution.py:152
  222.9 21.5 %all-to-all-start.3 = ((bf16[64,2,2048]{2,1,0:T(2,128)(2,1)}), bf16[64,2,2048]{2,1,0:T(2,128)(2,1)S(1)}, u32[]{:S(2)}, u32[]{:S(2)}) async-start(bf16[64,2,2048]{2,1,0:T(2,128)(2,1)} %reshape.1014), calls=%async_computation.3 | async-start | bytes 1048576 | tf_op jit(solution)/shard_map/all_to_all | solution.py:163
  231.9 75.1 %all-gather.5.cloned.1.call-start = ((), (), s32[]{:S(2)}) async-start(), calls=%async_computation.11 | async-start | bytes 1572864 | tf_op jit(solution)/shard_map/all_gather | solution.py:179
  281.1 5.1 copy-start.16
  284.0 49.4 %all-gather.3.cloned.1.call-start = ((), (), s32[]{:S(2)}) async-start(), calls=%async_computation.10 | async-start | bytes 1572864 | tf_op jit(solution)/shard_map/all_gather | solution.py:180
  286.1 91.7 %reduce-scatter.5.cloned.1.call-start = ((), (), s32[]{:S(2)}) async-start(), calls=%async_computation.13 | async-start | bytes 1572864 | tf_op jit(solution)/shard_map/reduce_scatter | solution.py:191
  341.8 5.1 copy-start.15
  353.9 50.1 %reduce-scatter.3.cloned.1.call-start = ((), (), s32[]{:S(2)}) async-start(), calls=%async_computation.12 | async-start | bytes 1572864 | tf_op jit(solution)/shard_map/reduce_scatter | solution.py:194
  424.6 20.8 %all-to-all-start.4 = ((bf16[64,2,2048]{2,1,0:T(2,128)(2,1)}), bf16[64,2,2048]{2,1,0:T(2,128)(2,1)S(1)}, u32[]{:S(2)}, u32[]{:S(2)}) async-start(bf16[64,2,2048]{2,1,0:T(2,128)(2,1)} %reshape.1016), calls=%async_computation.6 | async-start | bytes 1048576 | tf_op jit(solution)/shard_map/all_to_all | solution.py:203
  644.4 9.7 copy-start.11
  649.5 22.9 %all-to-all-start.6 = ((bf16[64,2,2048]{2,1,0:T(2,128)(2,1)}), bf16[64,2,2048]{2,1,0:T(2,128)(2,1)S(1)}, u32[]{:S(2)}, u32[]{:S(2)}) async-start(bf16[64,2,2048]{2,1,0:T(2,128)(2,1)} %reshape.1020), calls=%async_computation.8 | async-start | bytes 1048576 | tf_op jit(solution)/shard_map/all_to_all | solution.py:207
  666.2 15.6 %copy-start.22 = (bf16[1,16,64,384]{3,2,1,0:T(8,128)(2,1)S(1)}, bf16[1,16,64,384]{3,2,1,0:T(8,128)(2,1)}, u32[]{:S(2)}) copy-start(bf16[1,16,64,384]{3,2,1,0:T(8,128)(2,1)} %copy-done.21) | copy-start | bytes 2359300
  666.2 15.6 %copy-start.51 = (bf16[1,16,64,256]{3,2,1,0:T(8,128)(2,1)S(1)}, bf16[1,16,64,256]{3,2,1,0:T(8,128)(2,1)}, u32[]{:S(2)}) copy-start(bf16[1,16,64,256]{3,2,1,0:T(8,128)(2,1)} %reduce-scatter.3.cloned.1.call-done) | copy-start | bytes 1572868
  672.4 37.6 %all-to-all-start.7 = ((bf16[64,2,2048]{2,1,0:T(2,128)(2,1)}), bf16[64,2,2048]{2,1,0:T(2,128)(2,1)}, u32[]{:S(2)}, u32[]{:S(2)}) async-start(bf16[64,2,2048]{2,1,0:T(2,128)(2,1)} %reshape.1018), calls=%async_computation.9 | async-start | bytes 1048576 | tf_op jit(solution)/shard_map/all_to_all | solution.py:206
  710.0 44.3 %all-to-all-start.5 = ((bf16[64,2,2048]{2,1,0:T(2,128)(2,1)}), bf16[64,2,2048]{2,1,0:T(2,128)(2,1)S(1)}, u32[]{:S(2)}, u32[]{:S(2)}) async-start(bf16[64,2,2048]{2,1,0:T(2,128)(2,1)} %reshape.1022), calls=%async_computation.7 | async-start | bytes 1048576 | tf_op jit(solution)/shard_map/all_to_all | solution.py:208
  718.9 211.6 %all-reduce.21.cloned.1.call-start = ((), (), s32[]{:S(2)}) async-start(), calls=%async_computation.15 | async-start | bytes 6291456
  762.5 5.2 copy-start.20
  777.0 710.2 %all-reduce.19.cloned.1.call-start = ((), (), s32[]{:S(2)}) async-start(), calls=%async_computation.14 | async-start | bytes 6291456 | tf_op jit(solution)/shard_map/psum | solution.py:213
  930.4 560.6 %copy-start.1 = (bf16[16,128,384]{2,1,0:T(8,128)(2,1)S(1)}, bf16[16,128,384]{2,1,0:T(8,128)(2,1)}, u32[]{:S(2)}) copy-start(bf16[16,128,384]{2,1,0:T(8,128)(2,1)} %param.14) | copy-start | bytes 4718596
  (49 other events, 114.0 us)
Sparse Core Ops, SparseCore 0:
  284.1 22.8 all-gather.4
  308.6 24.7 all-gather.2
  354.0 23.7 reduce-scatter.4
  380.1 23.7 reduce-scatter.2
  777.0 153.3 all-reduce.20
  933.5 553.6 all-reduce.18
where the time goes:
time: 1510 us; the launch traced here: 1500 us
  waiting for transfers between devices  760 us (50%)
  local copies, waits for them, and re-layouts  238 us (16%)
  other arithmetic  235 us (16%)
  matrix products  185 us (12%)
  starting transfers between devices  63.9 us (4%)
  between operations  15.6 us (1%)
    psum x1, waiting for transfers between devices, shards(): band_grad = lax.psum(g_band, 'frames')  555 us
    unnamed x7, waiting for transfers between devices  144 us
    dot_general x24, matrix products, one_block(): return jnp.einsum('nts,nsd->ntd', probs, values_f).astype(jnp.bfloat16)  69 us
    dot_general x32, matrix products, block_weights(): scores = jnp.einsum('ntd,nsd->nts', lift(q_block), keys_f) * factor  67.5 us
    unnamed x121, local copies, waits for them, and re-layouts  46.8 us
    reduce_sum x24, other arithmetic, block_weights(): return jax.nn.softmax(scores, axis=-1).astype(jnp.bfloat16)  45.4 us
    another operation x12, other arithmetic  45.4 us
  transfers between devices with their start and end apart: 14, of which 10 were waited for; matrix products, arithmetic and copies ran while one was open for 12% of the time, Pallas kernels for 0%

commit v1 on v0

v1 whole, which is shorter than its diff:
```python
import math

import jax
import jax.numpy as jnp
import numpy as np
from jax import lax
from jax.experimental import pallas as pl
from jax.experimental.pallas import tpu as pltpu
from jax.sharding import PartitionSpec as P

EPS = 1e-05
THETA = 10000.0
NB = 32
NG = 16
NF = 64
ND = 128
FB = 64
HF = 32
T = 4096
D = 384
W = 128
BQ = 256
NQ = T // BQ
SAFE = 100.0 * 100.0
LOG2E = math.log2(math.e)
BF = jnp.bfloat16
F32 = jnp.float32
MESH = pl.DeviceIdType.MESH
VMEM_LIMIT = 60 * 1024 * 1024

NN = (((1,), (0,)), ((), ()))
NT = (((1,), (1,)), ((), ()))
TN = (((0,), (0,)), ((), ()))


def mm(a, b, dims=NN):
    return lax.dot_general(a, b, dims, preferred_element_type=F32)


def lanes(shape):
    return lax.broadcasted_iota(jnp.int32, shape, len(shape) - 1)


def swap_halves(x):
    lane = lanes(x.shape)
    ax = len(x.shape) - 1
    return jnp.where(lane % 64 < 32, pltpu.roll(x, 96, ax), pltpu.roll(x, 32, ax))


def rotary_tables(positions):
    i = np.arange(128) % 32
    freq = np.exp(i.astype(np.float64) * (-2.0 * math.log(THETA) / 64))
    sign = np.where(np.arange(128) % 64 < 32, -1.0, 1.0)
    ang = np.asarray(positions, np.float64)[:, None] * freq[None, :]
    return np.cos(ang).astype(np.float32), (np.sin(ang) * sign).astype(np.float32)


def prep_kernel(widths, spec, bw, feat, keep, send):
    bi = lax.axis_index("bands")
    start = jnp.int32(0)
    for j in range(NG):
        start = start + jnp.where(bi == 1, widths[j], 0)

    def one(k, start):
        w = widths[bi * NG + k]
        off = 2 * start
        blk = off // 128
        shift = off - blk * 128
        nxt = jnp.minimum(blk + 1, spec.shape[1] // 128 - 1)
        a = spec[:, pl.ds(pl.multiple_of(blk * 128, 128), 128)]
        b = spec[:, pl.ds(pl.multiple_of(nxt * 128, 128), 128)]
        x = jnp.concatenate([a, b], axis=1).astype(F32)
        y = pltpu.roll(x, lax.rem(256 - shift, 256), 1)[:, :128]
        y = jnp.where(lanes(y.shape) < 2 * w, y, 0.0).astype(BF)
        feat[k] = y
        lat = mm(y, bw[k]).astype(BF)

        @pl.when(bi == 0)
        def _():
            keep[k] = lat[:HF]
            send[k] = lat[HF:]

        @pl.when(bi == 1)
        def _():
            keep[k] = lat[HF:]
            send[k] = lat[:HF]

        return start + w

    lax.fori_loop(0, NG, one, start)


def angles_at(c, cc, sc, cr, sr):
    ca = cc[pl.ds(c, 1), :]
    sa = sc[pl.ds(c, 1), :]
    return ca * cr[...] - sa * sr[...], sa * cr[...] + ca * sr[...]


def normed_rows(feat_rows, bwk):
    lat = mm(feat_rows, bwk).astype(BF).astype(F32)
    r = lax.rsqrt(jnp.mean(lat * lat, axis=-1, keepdims=True) + EPS)
    return lat * r, r


def fwd_kernel(feat, bw, wh, cc, sc, cr, sr, e_out, q_out, k_out, v_out, ol_out, op_out, top):
    c = pl.program_id(0)
    band = lax.axis_index("frames") // 4

    @pl.when(c == 0)
    def _():
        top[...] = jnp.zeros_like(top)
        bwk = bw[band]

        def pre(j, _):
            rows = pl.ds(pl.multiple_of(j * BQ, BQ), BQ)
            n, _r = normed_rows(feat[rows, :], bwk)
            proj = mm(n.astype(BF), wh[...])
            co, si = angles_at(j, cc, sc, cr, sr)
            a = proj[:, :128]
            a = a * co + swap_halves(a) * si
            lane = lanes(a.shape)
            q = (a * jnp.where(lane < 64, 0.125 * LOG2E, 1.0)).astype(BF)
            qf = q.astype(F32)
            sq = qf * qf
            qn = jnp.max(jnp.sum(jnp.where(lane < 64, sq, 0.0), axis=1, keepdims=True))
            kn = jnp.max(jnp.sum(jnp.where(lane < 64, 0.0, sq), axis=1, keepdims=True))
            top[0:1, :] = jnp.maximum(top[0:1, :], qn)
            top[1:2, :] = jnp.maximum(top[1:2, :], kn)
            q_out[rows, :] = q
            k_out[rows, :] = jnp.where(lane < 64, pltpu.roll(qf, 64, 1), 0.0).astype(BF)
            v = jnp.concatenate([proj[:, 128:192], jnp.ones((BQ, 64), F32)], axis=1)
            v_out[rows, :] = v.astype(BF)
            return 0

        lax.fori_loop(0, NQ, pre, 0)

    rows = pl.ds(pl.multiple_of(c * BQ, BQ), BQ)
    q = q_out[rows, :]
    safe = jnp.max(top[0:1, :] * top[1:2, :]) < SAFE

    def finish(res):
        rl = 1.0 / res
        lane = lanes(res.shape)
        o = res * pltpu.roll(rl, 64, 1)
        ol_out[...] = jnp.where(lane < 64, o, rl)
        o4 = o.reshape(BQ // HF, 2, 16, 128)
        lane3 = lanes((BQ // HF, 16, 128))
        op_out[...] = jnp.where(lane3 < 64, o4[:, 0], pltpu.roll(o4[:, 1], 64, 2)).astype(BF)

    @pl.when(safe)
    def _():
        res = jnp.zeros((BQ, 128), F32)
        for j in range(8):
            cols = slice(j * 512, (j + 1) * 512)
            e = jnp.exp2(mm(q, k_out[cols, :], NT)).astype(BF)
            e_out[:, cols] = e
            res = res + mm(e, v_out[cols, :])
        finish(res)

    @pl.when(jnp.logical_not(safe))
    def _():
        s = mm(q, k_out[...], NT)
        e = jnp.exp2(s - jnp.max(s, axis=1, keepdims=True)).astype(BF)
        e_out[...] = e
        finish(mm(e, v_out[...]))


def bwd_kernel(e_in, feat, bw, wh, cc, sc, cr, sr, q_in, k_in, v_in, ol_in, dop, dsec, wrecv,
               gband, gq, wsum, dq_s, t_s, gb_s, gq_s):
    c = pl.program_id(0)
    fi = lax.axis_index("frames")
    rows = pl.ds(pl.multiple_of(c * BQ, BQ), BQ)

    @pl.when(c == 0)
    def _():
        t_s[...] = jnp.zeros_like(t_s)
        wsum[...] = jnp.sum(wrecv[...].astype(F32), axis=0)

    x = dop[...].astype(F32)
    do = jnp.concatenate([x[:, None], pltpu.roll(x, 64, 2)[:, None]], axis=1).reshape(BQ, 128)
    ol = ol_in[...]
    lane = lanes((BQ, 128))
    do = jnp.where(lane < 64, do * pltpu.roll(ol, 64, 1), 0.0)
    delta = jnp.sum(do * ol, axis=1, keepdims=True)
    hi = delta.astype(BF).astype(F32)
    aug = jnp.where(lane == 64, -hi, jnp.where(lane == 65, hi - delta, do)).astype(BF)
    do_t = do.T[:64].astype(BF)
    q_t = q_in[rows, :].astype(F32).T[:64].astype(BF)
    dq = jnp.zeros((BQ, 128), F32)
    for j in range(8):
        cols = slice(j * 512, (j + 1) * 512)
        e = e_in[:, cols]
        ds = (e.astype(F32) * mm(aug, v_in[cols, :], NT)).astype(BF)
        dq = dq + mm(ds, k_in[cols, :])
        t_s[0:64, cols] += mm(do_t, e)
        t_s[64:128, cols] += mm(q_t, ds)
    dq_s[rows, :] = dq * 0.125

    @pl.when(c == NQ - 1)
    def _():
        bwk = bw[fi // 4]
        gq_s[...] = jnp.zeros_like(gq_s)
        quarter = pl.ds(pl.multiple_of(lax.rem(fi, 4) * 1024, 1024), 1024)
        gb_s[...] = mm(feat[quarter, :], dsec[...], TN)

        def post(j, _):
            rows = pl.ds(pl.multiple_of(j * BQ, BQ), BQ)
            tx = t_s[:, rows].T
            a = jnp.where(lane < 64, dq_s[rows, :], tx * math.log(2.0)).astype(BF).astype(F32)
            co, si = angles_at(j, cc, sc, cr, sr)
            a = a * co - swap_halves(a) * si
            dproj = jnp.concatenate([a, tx[:, :64]], axis=1).astype(BF)
            dn = mm(dproj, wh[...], NT).astype(BF).astype(F32)
            f = feat[rows, :]
            n, r = normed_rows(f, bwk)
            dlat = (r * (dn - n * jnp.mean(n * dn, axis=1, keepdims=True))).astype(BF)
            gb_s[...] += mm(f, dlat, TN)
            gq_s[...] += mm(n.astype(BF), dproj, TN)
            return 0

        lax.fori_loop(0, NQ, post, 0)
        gband[...] = gb_s[...].reshape(4, 32, D).astype(BF)
        g = gq_s[...]
        g = jnp.concatenate([g, jnp.zeros((D, 64), F32)], axis=1)
        gq[...] = jnp.concatenate(
            [g[:, :128].reshape(48, 8, 128), g[:, 128:].reshape(48, 8, 128)], axis=1
        ).astype(BF)


def band_kernel(lat_own, lat_oth, cot_own, cot_oth, att, w_ot, w_qb, w_ob, cb, sb,
                lat_keep, lat_send, dsec_out, dop_out, wg_out,
                lat_s, cot_s, att_s, do_s, g_ot, g_qb, g_ob):
    bi = lax.axis_index("bands")
    own = pl.ds(pl.multiple_of(bi * 128, 128), 128)
    oth = pl.ds(pl.multiple_of((1 - bi) * 128, 128), 128)
    for ref, scr, where in ((lat_own, lat_s, own), (lat_oth, lat_s, oth), (cot_own, cot_s, own), (cot_oth, cot_s, oth)):
        x = ref[...].astype(F32)
        for g in range(4):
            scr[g, where, :] = x[:, 8 * g:8 * g + 8, :].reshape(128, D)
    lane = lanes((256, 128))
    low = lane < 64

    def pair(a, b, p):
        if p == 0:
            return jnp.where(low, a, pltpu.roll(b, 64, 1))
        return jnp.where(low, pltpu.roll(a, 64, 1), b)

    for j in range(2):
        x0 = att[:, 2 * j].astype(F32)
        x1 = att[:, 2 * j + 1].astype(F32)
        for g in range(4):
            p, rr = g // 2, g % 2
            a = x0[:, 8 * rr:8 * rr + 8, :].reshape(256, 128)
            b = x1[:, 8 * rr:8 * rr + 8, :].reshape(256, 128)
            att_s[g, :, 128 * j:128 * j + 128] = pair(a, b, p).astype(BF)

    g_ot[...] = jnp.zeros_like(g_ot)
    g_qb[...] = jnp.zeros_like(g_qb)
    g_ob[...] = jnp.zeros_like(g_ob)

    def group(g, _):
        att_g = att_s[g]
        cot = cot_s[g]
        cot_b = cot.astype(BF)
        sec = (lat_s[g] + mm(att_g, w_ot[...])).astype(BF).astype(F32)
        r = lax.rsqrt(jnp.mean(sec * sec, axis=-1, keepdims=True) + EPS)
        n = sec * r
        nb = n.astype(BF)
        proj = mm(nb, w_qb[...])
        dbatt = mm(cot_b, w_ob[...], NT)
        co, si = cb[...], sb[...]
        row_t = lax.broadcasted_iota(jnp.int32, (256, 256), 0) % 8
        col_t = lax.broadcasted_iota(jnp.int32, (256, 256), 1) % 8
        same = row_t == col_t
        batts, dqs, dks, dvs = [], [], [], []
        for j in range(2):
            q = proj[:, 128 * j:128 * j + 128]
            k = proj[:, 256 + 128 * j:384 + 128 * j]
            v = proj[:, 512 + 128 * j:640 + 128 * j].astype(BF)
            q = ((q * co + swap_halves(q) * si) * 0.125).astype(BF)
            k = (k * co + swap_halves(k) * si).astype(BF)
            do = dbatt[:, 128 * j:128 * j + 128].astype(BF)
            outs = []
            for hh in range(2):
                here = low if hh == 0 else jnp.logical_not(low)
                zero = jnp.zeros((), BF)
                qm = jnp.where(here, q, zero)
                dm = jnp.where(here, do, zero)
                s = jnp.where(same, mm(qm, k, NT), -jnp.inf)
                e = jnp.exp(s - jnp.max(s, axis=1, keepdims=True))
                p = e * (1.0 / jnp.sum(e, axis=1, keepdims=True))
                pb = p.astype(BF)
                pf = pb.astype(F32)
                o = mm(pb, v)
                dp = mm(dm, v, NT)
                ds = (pf * (dp - jnp.sum(pf * dp, axis=1, keepdims=True))).astype(BF)
                outs.append((o, mm(ds, k), mm(ds, q, TN), mm(pb, do, TN)))
            batts.append(jnp.where(low, outs[0][0], outs[1][0]).astype(BF))
            dq = (jnp.where(low, outs[0][1], outs[1][1]) * 0.125).astype(BF).astype(F32)
            dk = jnp.where(low, outs[0][2], outs[1][2]).astype(BF).astype(F32)
            dqs.append((dq * co - swap_halves(dq) * si).astype(BF))
            dks.append((dk * co - swap_halves(dk) * si).astype(BF))
            dvs.append(jnp.where(low, outs[0][3], outs[1][3]).astype(BF))
        batt = jnp.concatenate(batts, axis=1)
        dproj = jnp.concatenate(dqs + dks + dvs, axis=1)
        lat_s[g] = sec + mm(batt, w_ob[...])
        dn = mm(dproj, w_qb[...], NT).astype(BF).astype(F32)
        dsec = (cot + r * (dn - n * jnp.mean(n * dn, axis=1, keepdims=True))).astype(BF)
        cot_s[g] = dsec.astype(F32)
        do_s[g] = mm(dsec, w_ot[...], NT)
        g_ob[...] += mm(batt, cot_b, TN)
        g_qb[...] += mm(nb, dproj, TN)
        g_ot[...] += mm(att_g, dsec, TN)
        return 0

    lax.fori_loop(0, 4, group, 0)

    for ref, where in ((lat_keep, own), (lat_send, oth)):
        ref[...] = jnp.concatenate(
            [lat_s[g, where, :].reshape(NG, 8, D) for g in range(4)], axis=1
        ).astype(BF)
    dsec_out[...] = jnp.concatenate(
        [cot_s[g].reshape(NB, 8, D) for g in range(4)], axis=1
    ).astype(BF)
    for j in range(2):
        for hh in range(2):
            parts = []
            for rr in range(2):
                a = do_s[rr, :, 128 * j:128 * j + 128]
                b = do_s[2 + rr, :, 128 * j:128 * j + 128]
                parts.append(pair(a, b, hh).reshape(NB, 8, 128))
            dop_out[:, 2 * j + hh] = jnp.concatenate(parts, axis=1).astype(BF)
    wg_out[0:16] = g_ot[...].reshape(16, 16, D).astype(BF)
    wg_out[16:64] = jnp.concatenate(
        [g_qb[:, :D].reshape(48, 8, D), g_qb[:, D:].reshape(48, 8, D)], axis=1
    ).astype(BF)
    wg_out[64:80] = g_ob[...].reshape(16, 16, D).astype(BF)


def here():
    return lax.axis_index("frames"), lax.axis_index("bands")


def group_barrier():
    fi, bi = here()
    sem = pltpu.get_barrier_semaphore()

    def body(d, _):
        pl.semaphore_signal(sem, inc=1, device_id=(lax.rem(fi + d, NF), bi), device_id_type=MESH)
        return 0

    lax.fori_loop(1, NF, body, 0)
    pl.semaphore_wait(sem, NF - 1)


def full_barrier():
    fi, bi = here()
    me = fi * 2 + bi
    sem = pltpu.get_barrier_semaphore()

    def body(d, _):
        t = lax.rem(me + d, ND)
        pl.semaphore_signal(sem, inc=1, device_id=(t // 2, lax.rem(t, 2)), device_id_type=MESH)
        return 0

    lax.fori_loop(1, ND, body, 0)
    pl.semaphore_wait(sem, ND - 1)


def wait_bytes(ref, sem):
    pltpu.make_async_copy(ref, ref, sem).wait()


def send_feat_kernel(src, dst, send_sem, recv_sem):
    fi, bi = here()
    group_barrier()
    pltpu.make_async_copy(src.at[fi // 4], dst.at[fi], recv_sem).start()

    def body(d, _):
        t = lax.rem(fi + d, NF)
        pltpu.make_async_remote_copy(
            src.at[t // 4], dst.at[fi], send_sem, recv_sem, device_id=(t, bi), device_id_type=MESH
        ).start()
        return 0

    lax.fori_loop(1, NF, body, 0)
    wait_bytes(dst, recv_sem)
    wait_bytes(dst.at[pl.ds(0, NF - 1)], send_sem)


def send_att_kernel(src, dst, send_sem, recv_sem):
    fi, bi = here()
    me = fi * 2 + bi
    slot = bi * NF + fi
    full_barrier()
    pltpu.make_async_copy(src.at[me], dst.at[slot], recv_sem).start()

    def body(d, _):
        t = lax.rem(me + d, ND)
        pltpu.make_async_remote_copy(
            src.at[t], dst.at[slot], send_sem, recv_sem,
            device_id=(t // 2, lax.rem(t, 2)), device_id_type=MESH,
        ).start()
        return 0

    lax.fori_loop(1, ND, body, 0)
    wait_bytes(dst, recv_sem)
    wait_bytes(dst.at[pl.ds(0, ND - 1)], send_sem)


def send_back_kernel(dop, dsec, wg, dop_r, dsec_r, wg_r, send_sems, recv_sems):
    fi, bi = here()
    me = fi * 2 + bi
    slot = bi * NF + fi
    full_barrier()
    pltpu.make_async_copy(dop.at[slot], dop_r.at[me], recv_sems.at[0]).start()

    def body(d, _):
        t = lax.rem(slot + d, ND)
        pltpu.make_async_remote_copy(
            dop.at[t], dop_r.at[me], send_sems.at[0], recv_sems.at[0],
            device_id=(lax.rem(t, NF), t // NF), device_id_type=MESH,
        ).start()
        return 0

    lax.fori_loop(1, ND, body, 0)

    quarter = fi // 16
    place = lax.rem(fi, 16) * 2 + bi
    selfish = lax.rem(fi, 4) == quarter

    def body2(k, _):
        f, b = lax.rem(k, NG) * 4 + quarter, k // NG
        is_self = jnp.logical_and(f == fi, b == bi)

        @pl.when(is_self)
        def _():
            pltpu.make_async_copy(dsec.at[k], dsec_r.at[place], recv_sems.at[1]).start()

        @pl.when(jnp.logical_not(is_self))
        def _():
            pltpu.make_async_remote_copy(
                dsec.at[k], dsec_r.at[place], send_sems.at[1], recv_sems.at[1],
                device_id=(f, b), device_id_type=MESH,
            ).start()

        return 0

    lax.fori_loop(0, NB, body2, 0)

    def body3(d, _):
        is_self = d == me

        @pl.when(is_self)
        def _():
            pltpu.make_async_copy(wg.at[d - 48], wg_r.at[me], recv_sems.at[2]).start()

        @pl.when(jnp.logical_not(is_self))
        def _():
            pltpu.make_async_remote_copy(
                wg.at[d - 48], wg_r.at[me], send_sems.at[2], recv_sems.at[2],
                device_id=(d // 2, lax.rem(d, 2)), device_id_type=MESH,
            ).start()

        return 0

    lax.fori_loop(48, ND, body3, 0)

    wait_bytes(dop_r, recv_sems.at[0])
    wait_bytes(dop.at[pl.ds(0, ND - 1)], send_sems.at[0])
    wait_bytes(dsec_r, recv_sems.at[1])
    wait_bytes(dsec.at[pl.ds(0, NB - 1)], send_sems.at[1])

    @pl.when(jnp.logical_not(selfish))
    def _():
        wait_bytes(dsec.at[0], send_sems.at[1])

    wait_bytes(wg.at[pl.ds(0, 79)], send_sems.at[2])

    @pl.when(me >= 48)
    def _():
        wait_bytes(wg_r, recv_sems.at[2])

    @pl.when(me < 48)
    def _():
        wait_bytes(wg.at[0], send_sems.at[2])


def tail_kernel(gband, gq, out, gsum, quad, part, gq_r, send_sems, recv_sems):
    fi, bi = here()
    me = fi * 2 + bi
    full_barrier()
    mine = lax.rem(fi, 4)
    base = fi - mine
    pltpu.make_async_copy(gband.at[mine], quad.at[mine], recv_sems.at[0]).start()
    for d in range(1, 4):
        t = lax.rem(mine + d, 4)
        pltpu.make_async_remote_copy(
            gband.at[t], quad.at[mine], send_sems.at[0], recv_sems.at[0],
            device_id=(base + t, bi), device_id_type=MESH,
        ).start()

    def body(d, _):
        is_self = d == me

        @pl.when(is_self)
        def _():
            pltpu.make_async_copy(gq.at[d], gq_r.at[me], recv_sems.at[1]).start()

        @pl.when(jnp.logical_not(is_self))
        def _():
            pltpu.make_async_remote_copy(
                gq.at[d], gq_r.at[me], send_sems.at[1], recv_sems.at[1],
                device_id=(d // 2, lax.rem(d, 2)), device_id_type=MESH,
            ).start()

        return 0

    lax.fori_loop(0, 48, body, 0)

    wait_bytes(quad, recv_sems.at[0])
    part[...] = jnp.sum(quad[...].astype(F32), axis=0).astype(BF)
    pltpu.make_async_copy(part, out.at[fi], recv_sems.at[2]).start()

    def body2(d, _):
        pltpu.make_async_remote_copy(
            part, out.at[fi], send_sems.at[2], recv_sems.at[2],
            device_id=(lax.rem(fi + d, NF), bi), device_id_type=MESH,
        ).start()
        return 0

    lax.fori_loop(1, NF, body2, 0)

    @pl.when(me < 48)
    def _():
        wait_bytes(gq_r, recv_sems.at[1])
        x = gq_r[...].reshape(NG, 4, 2, 16, 128)
        gsum[...] = jnp.sum(x.astype(F32), axis=(0, 2))

    @pl.when(me >= 48)
    def _():
        gsum[...] = jnp.zeros_like(gsum)

    wait_bytes(out, recv_sems.at[2])
    wait_bytes(gband.at[pl.ds(0, 3)], send_sems.at[0])
    wait_bytes(gq.at[pl.ds(0, 47)], send_sems.at[1])

    @pl.when(me >= 48)
    def _():
        wait_bytes(gq.at[0], send_sems.at[1])

    wait_bytes(out.at[pl.ds(0, NF - 1)], send_sems.at[2])


VM = pl.BlockSpec(memory_space=pltpu.VMEM)
SM = pl.BlockSpec(memory_space=pltpu.SMEM)
ANY = pl.BlockSpec(memory_space=pl.ANY)


def struct(shape, dtype):
    return jax.ShapeDtypeStruct(shape, dtype)


def remote(kernel, outs, cid, n_sem, args, out_specs=None, in_specs=None, scratch=()):
    shape = (n_sem,) if n_sem else ()
    return pl.pallas_call(
        kernel,
        out_shape=outs,
        in_specs=in_specs or [ANY] * len(args),
        out_specs=out_specs or ([ANY] * len(outs) if isinstance(outs, list) else ANY),
        scratch_shapes=list(scratch) + [pltpu.SemaphoreType.DMA(shape), pltpu.SemaphoreType.DMA(shape)],
        compiler_params=pltpu.CompilerParams(
            collective_id=cid, has_side_effects=True, vmem_limit_bytes=VMEM_LIMIT
        ),
    )(*args)


def whole(shape):
    return pl.BlockSpec(shape, lambda c: (0,) * len(shape))


def shards(spectrum, band_widths, band_weight, qkv_time, out_time, qkv_band, out_band, cotangent):
    fi, bi = here()
    me = fi * 2 + bi
    swap = [(0, 1), (1, 0)]
    head = lax.rem(fi, 4)

    cot = cotangent[0]
    cot_own = lax.dynamic_slice_in_dim(cot, bi * HF, HF, 1)
    cot_oth = lax.ppermute(lax.dynamic_slice_in_dim(cot, (1 - bi) * HF, HF, 1), "bands", swap)

    feat_own, lat_own, lat_away = pl.pallas_call(
        prep_kernel,
        out_shape=[struct((NG, FB, W), BF), struct((NG, HF, D), BF), struct((NG, HF, D), BF)],
        in_specs=[SM, VM, VM],
        out_specs=[VM, VM, VM],
        compiler_params=pltpu.CompilerParams(vmem_limit_bytes=VMEM_LIMIT),
    )(band_widths, spectrum[0], band_weight)

    feat = remote(send_feat_kernel, struct((NF, FB, W), BF), 1, 0, (feat_own,)).reshape(T, W)
    lat_oth = lax.ppermute(lat_away, "bands", swap)

    wh = lax.dynamic_index_in_dim(qkv_time.reshape(D, 3, 4, 64), head, 2, keepdims=False).reshape(D, 192)
    cc, sc = rotary_tables(np.arange(NQ) * BQ)
    cr, sr = rotary_tables(np.arange(BQ))
    tables = tuple(jnp.asarray(x) for x in (cc, sc, cr, sr))
    table_specs = [whole((NQ, 128)), whole((NQ, 128)), whole((BQ, 128)), whole((BQ, 128))]
    params = pltpu.CompilerParams(
        dimension_semantics=("arbitrary",), vmem_limit_bytes=VMEM_LIMIT
    )

    e, q, k, v, ol, op = pl.pallas_call(
        fwd_kernel,
        grid=(NQ,),
        out_shape=[struct((T, T), BF), struct((T, 128), BF), struct((T, 128), BF), struct((T, 128), BF),
                   struct((T, 128), F32), struct((ND, 16, 128), BF)],
        in_specs=[whole((T, W)), whole((NG, W, D)), whole((D, 192))] + table_specs,
        out_specs=[pl.BlockSpec((BQ, T), lambda c: (c, 0)), whole((T, 128)), whole((T, 128)), whole((T, 128)),
                   pl.BlockSpec((BQ, 128), lambda c: (c, 0)), pl.BlockSpec((8, 16, 128), lambda c: (c, 0, 0))],
        scratch_shapes=[pltpu.VMEM((8, 128), F32)],
        compiler_params=params,
        cost_estimate=pl.CostEstimate(flops=2 * 2 * T * T * 256, bytes_accessed=2 * T * T, transcendentals=T * T),
    )(feat, band_weight, wh, *tables)

    att = remote(send_att_kernel, struct((ND, 16, 128), BF), 2, 0, (op,)).reshape(NB, 4, 16, 128)

    cb, sb = rotary_tables(np.arange(256) // 8)
    lat_keep, lat_send, dsec, dop, wg = pl.pallas_call(
        band_kernel,
        out_shape=[struct((NG, HF, D), BF), struct((NG, HF, D), BF), struct((NB, HF, D), BF),
                   struct((NB, 4, 16, 128), BF), struct((80, 16, D), BF)],
        in_specs=[VM] * 10,
        out_specs=[VM] * 5,
        scratch_shapes=[pltpu.VMEM((4, 256, D), F32), pltpu.VMEM((4, 256, D), F32), pltpu.VMEM((4, 256, 256), BF),
                        pltpu.VMEM((4, 256, 256), F32), pltpu.VMEM((256, D), F32), pltpu.VMEM((D, 768), F32),
                        pltpu.VMEM((256, D), F32)],
        compiler_params=pltpu.CompilerParams(vmem_limit_bytes=VMEM_LIMIT),
    )(lat_own, lat_oth, cot_own, cot_oth, att, out_time, qkv_band, out_band, jnp.asarray(cb), jnp.asarray(sb))

    lat_recv = lax.ppermute(lat_send, "bands", swap)
    dop_r, dsec_r, wg_r = remote(
        send_back_kernel,
        [struct((ND, 16, 128), BF), struct((NB, HF, D), BF), struct((ND, 16, D), BF)],
        3, 3, (dop.reshape(ND, 16, 128), dsec, wg),
    )

    gband, gq, wsum = pl.pallas_call(
        bwd_kernel,
        grid=(NQ,),
        out_shape=[struct((4, 32, D), BF), struct((48, 16, 128), BF), struct((16, D), F32)],
        in_specs=[pl.BlockSpec((BQ, T), lambda c: (c, 0)), whole((T, W)), whole((NG, W, D)), whole((D, 192))]
        + table_specs
        + [whole((T, 128)), whole((T, 128)), whole((T, 128)), pl.BlockSpec((BQ, 128), lambda c: (c, 0)),
           pl.BlockSpec((8, 16, 128), lambda c: (c, 0, 0)), whole((1024, D)), whole((ND, 16, D))],
        out_specs=[whole((4, 32, D)), whole((48, 16, 128)), whole((16, D))],
        scratch_shapes=[pltpu.VMEM((T, 128), F32), pltpu.VMEM((128, T), F32), pltpu.VMEM((W, D), F32),
                        pltpu.VMEM((D, 192), F32)],
        compiler_params=params,
        cost_estimate=pl.CostEstimate(flops=4 * 2 * T * T * 256, bytes_accessed=2 * T * T, transcendentals=0),
    )(e, feat, band_weight, wh, *tables, q, k, v, ol, dop_r, dsec_r.reshape(1024, D), wg_r)

    out, gsum = remote(
        tail_kernel,
        [struct((NF, 32, D), BF), struct((4, 16, 128), F32)],
        4, 3, (gband, gq),
        in_specs=[VM, VM],
        out_specs=[VM, VM],
        scratch=[pltpu.VMEM((4, 32, D), BF), pltpu.VMEM((32, D), BF), pltpu.VMEM((ND, 16, 128), BF)],
    )
    band_grad = out.reshape(NG, W, D).astype(F32)

    lat_lo = jnp.where(bi == 0, lat_keep, lat_recv)
    lat_hi = jnp.where(bi == 0, lat_recv, lat_keep)
    latent = jnp.concatenate([lat_lo, lat_hi], axis=1)[None]

    gt = jnp.stack([gsum[:, :8, :64], gsum[:, :8, 64:], gsum[:, 8:, :64]])
    share_t = gt.transpose(2, 0, 1, 3).reshape(-1)
    share_q = wsum.reshape(2, 8, D).transpose(1, 0, 2).reshape(-1)
    share = jnp.where(me < 48, share_t, jnp.where((me >= 64) & (me < 112), share_q, wsum.reshape(-1)))
    return (latent, band_grad, share)


def solution(mesh):
    placed = (
        P(None, "frames", None),
        P(),
        P("bands", None, None),
        P(),
        P(),
        P(),
        P(),
        P(None, "bands", "frames", None),
    )
    return jax.shard_map(
        shards,
        mesh=mesh,
        in_specs=placed,
        out_specs=(
            P(None, "bands", "frames", None),
            P("bands", None, None),
            P(("frames", "bands")),
        ),
        check_vma=False,
    )
```

time: 1510 us -> 292 us (0.19)
  waiting for transfers between devices: 760 us -> 0.01 us
  Pallas kernels: 0 us -> 274 us
  local copies, waits for them, and re-layouts: 238 us -> 6.57 us
  other arithmetic: 235 us -> 5.16 us
  matrix products: 185 us -> 0 us
  starting transfers between devices: 63.9 us -> 4.96 us
    psum x1 -> x0, waiting for transfers between devices: 555 us -> none  [shards(): band_grad = lax.psum(g_band, 'frames')]
    pallas_call x0 -> x8, Pallas kernels: none -> 274 us  [the longest x4 138 us: remote(): pl.pallas_call(kernel, out_shape=outs, in_specs=in_specs or [ANY] * len(a...]
    dot_general x75 -> x0, matrix products: 179 us -> none  [the longest x24 69 us: one_block(): return jnp.einsum('nts,nsd->ntd', probs, values_f).astype(jnp.bfloat16)]
    unnamed x7 -> x0, waiting for transfers between devices: 144 us -> none
    all_to_all x8 -> x0, starting transfers between devices: 63.6 us -> none  [the longest x1 10.9 us: shards(): lax.all_to_all(t_key, 'frames', split_axis=0, concat_axis=1, tiled=True)]
    reduce_sum x29 -> x0, other arithmetic: 47.8 us -> none  [the longest x24 45.4 us: block_weights(): return jax.nn.softmax(scores, axis=-1).astype(jnp.bfloat16)]
    reshape x23 -> x5, local copies, waits for them, and re-layouts: 48.9 us -> 2.42 us  [the longest x1 0.82 us: shards(): lax.dynamic_index_in_dim(qkv_time.reshape(D, 3, 4, 64), head, 2, keepdims...]
    unnamed x121 -> x9, local copies, waits for them, and re-layouts: 46.8 us -> 1.21 us
  transfers between devices with their start and end apart: 14 -> 3, of which waited for: 10 -> 0; matrix products, arithmetic and copies ran while one was open for 12% -> 3% of each run, Pallas kernels for 0% -> 87%
where the time goes in v1:
time: 292 us; the launch traced here: 291 us
  Pallas kernels  274 us (94%)
  local copies, waits for them, and re-layouts  6.57 us (2%)
  other arithmetic  5.16 us (2%)
  starting transfers between devices  4.96 us (2%)
    pallas_call x4, Pallas kernels, remote(): pl.pallas_call(kernel, out_shape=outs, in_specs=in_specs or [ANY] * len(a...  138 us
    pallas_call x1, Pallas kernels, shards(): pl.pallas_call(bwd_kernel, grid=(NQ,), out_shape=[struct((4, 32, D), BF),...  67.1 us
    pallas_call x1, Pallas kernels, shards(): pl.pallas_call(fwd_kernel, grid=(NQ,), out_shape=[struct((T, T), BF), str...  43.4 us
    pallas_call x1, Pallas kernels, shards(): pl.pallas_call(band_kernel, out_shape=[struct((NG, HF, D), BF), struct((N...  19.8 us
    pallas_call x1, Pallas kernels, shards(): pl.pallas_call(prep_kernel, out_shape=[struct((NG, FB, W), BF), struct((N...  6.04 us
  transfers between devices with their start and end apart: 3, of which 0 were waited for; matrix products, arithmetic and copies ran while one was open for 3% of the time, Pallas kernels for 87%

profile of v1, /device:TPU:1, one launch (start us, length us, event | category | flops | bytes accessed | tf_op | source)
XLA Modules:
  0.0 291.4 jit_solution(5486029572675047661)
XLA Ops:
  0.6 2.0 dynamic-slice_bitcast_fusion
  2.7 3.6 %collective-permute-start.1 = (bf16[16,32,384]{2,1,0:T(8,128)(2,1)S(1)}, bf16[16,32,384]{2,1,0:T(8,128)(2,1)S(1)}, u32[]{:S(2)}, u32[]{:S(2)}) collective-permute-start(bf16[16,32,384]{2,1,0:T(8,128)(2,1)S(1)} %get-tuple-element.49), channel_id=1, source_target_pairs={{0,1},{1,0},{2,3},{3,2},{4,5},{5,4},{6,7},{7,6},{8,9},{9,8},{10,11... | collective-permute-start | bytes 1179656 | tf_op jit(solution)/shard_map/ppermute | solution.py:590
  6.3 6.0 %shard_map.157 = (bf16[16,64,128]{2,1,0:T(8,128)(2,1)}, bf16[16,32,384]{2,1,0:T(8,128)(2,1)}, bf16[16,32,384]{2,1,0:T(8,128)(2,1)}) custom-call(s32[32]{0:T(128)} %widths.1, bf16[64,1280]{1,0:T(8,128)(2,1)} %bitcast.36, bf16[16,128,384]{2,1,0:T(8,128)(2,1)} %bw.5), custom_call_target="tpu_custom_call" | custom-call | tf_op jit(solution)/shard_map/pallas_call | solution.py:592
  12.3 0.0 collective-permute-start
  12.3 0.3 copy.18
  12.6 0.8 copy.19.wh
  13.5 23.8 %shard_map.158 = bf16[64,64,128]{2,1,0:T(8,128)(2,1)} custom-call(bf16[16,64,128]{2,1,0:T(8,128)(2,1)} %get-tuple-element.27.src), custom_call_target="tpu_custom_call" | custom-call | tf_op jit(solution)/shard_map/pallas_call | solution.py:566
  37.3 43.4 %shard_map.159 = (bf16[4096,4096]{1,0:T(8,128)(2,1)}, bf16[4096,128]{1,0:T(8,128)(2,1)}, bf16[4096,128]{1,0:T(8,128)(2,1)}, bf16[4096,128]{1,0:T(8,128)(2,1)}, f...) custom-call(bf16[4096,128]{1,0:T(8,128)(2,1)} %bitcast.31, bf16[16,128,384]{2,1,0:T(8,128)(2,1)} %bw.5, ...), custom_call_target="tpu_custom_call" | custom-call | flops 17179869184 | bytes 33554432 | tf_op jit(solution)/shard_map/pallas_call | solution.py:612
  80.7 19.6 %shard_map.160 = bf16[128,16,128]{2,1,0:T(8,128)(2,1)} custom-call(bf16[128,16,128]{2,1,0:T(8,128)(2,1)} %get-tuple-element.28.src), custom_call_target="tpu_custom_call" | custom-call | tf_op jit(solution)/shard_map/pallas_call | solution.py:566
  100.3 0.7 copy-done.1
  101.1 0.2 copy-done.2
  101.2 19.8 %shard_map.161 = (bf16[16,32,384]{2,1,0:T(8,128)(2,1)}, bf16[16,32,384]{2,1,0:T(8,128)(2,1)}, bf16[32,32,384]{2,1,0:T(8,128)(2,1)}, bf16[32,4,16,128]{3,2,1,0:T(8,128)(2,1)}, bf16[80,16,384]{2,1,0:T(8,128)(2,1)}) custom-call(bf16[16,32,384]{2,1,0:T(8,128)(2,1)} %get-tuple-element.25.lat_own, bf16[16,32,384]{2,1,0:T(8,128)(2,1)} %copy-done.2, ...), custom_call_target="tpu_custom_call" | custom-call | tf_op jit(solution)/shard_map/pallas_call | solution.py:628
  121.1 1.4 collective-permute-start.2
  122.5 48.6 %shard_map.162 = (bf16[128,16,128]{2,1,0:T(8,128)(2,1)}, bf16[32,32,384]{2,1,0:T(8,128)(2,1)}, bf16[128,16,384]{2,1,0:T(8,128)(2,1)}) custom-call(bf16[128,16,128]{2,1,0:T(8,128)(2,1)} %bitcast.35, bf16[32,32,384]{2,1,0:T(8,128)(2,1)} %get-tuple-element.37.dsec, bf16[80,16,384]{2,1,0:T(8,128)(2,1)} %get-tuple-element.38.wg), custom_call_target="tpu_custom_call" | custom-call | tf_op jit(solution)/shard_map/pallas_call | solution.py:566
  171.1 67.1 %shard_map.163 = (bf16[4,32,384]{2,1,0:T(8,128)(2,1)}, bf16[48,16,128]{2,1,0:T(8,128)(2,1)}, f32[16,384]{1,0:T(8,128)}) custom-call(bf16[4096,4096]{1,0:T(8,128)(2,1)} %get-tuple-element.31.e_in, bf16[4096,128]{1,0:T(8,128)(2,1)} %bitcast.32, bf16[16,128,384]{2,1,0:T(8,128)(2,1)} %bw.5, bf16[384,192]{1,0:T(8,128)(2,1)} %copy.19.wh, ...), custom_call_target="tpu_custom_call" | custom-call | flops 34359738368 | bytes 33554432 | tf_op jit(solution)/shard_map/pallas_call | solution.py:647
  238.2 0.7 reshape.51
  239.0 0.8 copy.24
  239.7 45.5 %shard_map.164 = (bf16[64,32,384]{2,1,0:T(8,128)(2,1)}, f32[4,16,128]{2,1,0:T(8,128)}) custom-call(bf16[4,32,384]{2,1,0:T(8,128)(2,1)} %get-tuple-element.42.gband, bf16[48,16,128]{2,1,0:T(8,128)(2,1)} %get-tuple-element.43.gq), custom_call_target="tpu_custom_call" | custom-call | tf_op jit(solution)/shard_map/pallas_call | solution.py:566
  285.2 0.9 slice_bitcast_fusion.2
  286.1 0.1 reshape.48
  286.2 0.6 select_select_fusion
  286.8 3.5 %bitcast_convert_fusion = f32[16,128,384]{2,1,0:T(8,128)} fusion(bf16[16,128,384]{2,1,0:T(8,128)(2,1)} %bitcast.30), kind=kLoop, calls=%fused_computation | loop fusion | flops 786432 | bytes 4718592 | tf_op jit(solution)/shard_map/convert_element_type | solution.py:670
  290.3 0.1 broadcast_select_fusion.1
  290.4 1.0 maximum_bitcast_fusion
  (13 shorter events, 0.1 us)
Async XLA Ops:
  0.6 11.7 %copy-start = (bf16[384,768]{1,0:T(8,128)(2,1)S(1)}, bf16[384,768]{1,0:T(8,128)(2,1)}, u32[]{:S(2)}) copy-start(bf16[384,768]{1,0:T(8,128)(2,1)} %param.17) | copy-start | bytes 1769476
  2.7 97.6 %collective-permute-start.1 = (bf16[16,32,384]{2,1,0:T(8,128)(2,1)S(1)}, bf16[16,32,384]{2,1,0:T(8,128)(2,1)S(1)}, u32[]{:S(2)}, u32[]{:S(2)}) collective-permute-start(bf16[16,32,384]{2,1,0:T(8,128)(2,1)S(1)} %get-tuple-element.49), channel_id=1, source_target_pairs={{0,1},{1,0},{2,3},{3,2},{4,5},{5,4},{6,7},{7,6},{8,9},{9,8},{10,11... | collective-permute-start | bytes 1179656 | tf_op jit(solution)/shard_map/ppermute | solution.py:590
  12.3 88.0 %collective-permute-start = (bf16[16,32,384]{2,1,0:T(8,128)(2,1)}, bf16[16,32,384]{2,1,0:T(8,128)(2,1)S(1)}, u32[]{:S(2)}, u32[]{:S(2)}) collective-permute-start(bf16[16,32,384]{2,1,0:T(8,128)(2,1)} %get-tuple-element.26), channel_id=1, source_target_pairs={{0,1},{1,0},{2,3},{3,2},{4,5},{5,4},{6,7},{7,6},{8,9},{9,8},{10,11... | collective-permute-start | bytes 1179656 | tf_op jit(solution)/shard_map/ppermute | solution.py:601
  100.3 0.8 copy-start.1
  100.3 0.9 copy-start.2
  121.1 169.2 %collective-permute-start.2 = (bf16[16,32,384]{2,1,0:T(8,128)(2,1)}, bf16[16,32,384]{2,1,0:T(8,128)(2,1)S(1)}, u32[]{:S(2)}, u32[]{:S(2)}) collective-permute-start(bf16[16,32,384]{2,1,0:T(8,128)(2,1)} %get-tuple-element.30), channel_id=1, source_target_pairs={{0,1},{1,0},{2,3},{3,2},{4,5},{5,4},{6,7},{7,6},{8,9},{9,8},{10,11... | collective-permute-start | bytes 1179656 | tf_op jit(solution)/shard_map/ppermute | solution.py:640
  286.8 3.5 %copy-start.3 = (bf16[16,32,384]{2,1,0:T(8,128)(2,1)S(1)}, bf16[16,32,384]{2,1,0:T(8,128)(2,1)}, u32[]{:S(2)}) copy-start(bf16[16,32,384]{2,1,0:T(8,128)(2,1)} %get-tuple-element.29) | copy-start | bytes 1179652

commit v2 on v0

v2 whole, which is shorter than its diff:
```python
import math

import jax
import jax.numpy as jnp
import numpy as np
from jax import lax
from jax.experimental import pallas as pl
from jax.experimental.pallas import tpu as pltpu
from jax.sharding import PartitionSpec as P

EPS = 1e-05
THETA = 10000.0
NB = 32
NG = 16
NF = 64
ND = 128
FB = 64
HF = 32
T = 4096
D = 384
W = 128
BQ = 256
NQ = T // BQ
CF = 512
CB = 1024
LOG2E = math.log2(math.e)
BF = jnp.bfloat16
F32 = jnp.float32
MESH = pl.DeviceIdType.MESH
VMEM_LIMIT = 63 * 1024 * 1024

NN = (((1,), (0,)), ((), ()))
NT = (((1,), (1,)), ((), ()))
TN = (((0,), (0,)), ((), ()))


def mm(a, b, dims=NN):
    return lax.dot_general(a, b, dims, preferred_element_type=F32)


def lanes(shape):
    return lax.broadcasted_iota(jnp.int32, shape, len(shape) - 1)


def swap_halves(x):
    lane = lanes(x.shape)
    ax = len(x.shape) - 1
    return jnp.where(lane % 64 < 32, pltpu.roll(x, 96, ax), pltpu.roll(x, 32, ax))


def rotary_tables(positions):
    i = np.arange(128) % 32
    freq = np.exp(i.astype(np.float64) * (-2.0 * math.log(THETA) / 64))
    sign = np.where(np.arange(128) % 64 < 32, -1.0, 1.0)
    ang = np.asarray(positions, np.float64)[:, None] * freq[None, :]
    return np.cos(ang).astype(np.float32), (np.sin(ang) * sign).astype(np.float32)


def here():
    return lax.axis_index("frames"), lax.axis_index("bands")


def wait_bytes(ref, sem):
    pltpu.make_async_copy(ref, ref, sem).wait()


def copy_to(src, dst, send_sem, recv_sem, frames, bands):
    pltpu.make_async_remote_copy(
        src, dst, send_sem, recv_sem, device_id=(frames, bands), device_id_type=MESH
    ).start()


def copy_out(src, dst, send_sem, recv_sem, frames, bands):
    fi, bi = here()
    mine = jnp.logical_and(frames == fi, bands == bi)

    @pl.when(mine)
    def _():
        pltpu.make_async_copy(src, dst, recv_sem).start()

    @pl.when(jnp.logical_not(mine))
    def _():
        copy_to(src, dst, send_sem, recv_sem, frames, bands)


def loop(lo, hi, body):
    def step(i, carry):
        body(i)
        return carry

    lax.fori_loop(lo, hi, step, 0)


def rows_of(j, n=BQ):
    return pl.ds(pl.multiple_of(j * n, n), n)


def angles_at(c, cc, sc, cr, sr):
    ca = cc[pl.ds(c, 1), :]
    sa = sc[pl.ds(c, 1), :]
    return ca * cr[...] - sa * sr[...], sa * cr[...] + ca * sr[...]


def normed_rows(feat_rows, bwk):
    lat = mm(feat_rows, bwk).astype(BF).astype(F32)
    r = lax.rsqrt(jnp.mean(lat * lat, axis=-1, keepdims=True) + EPS)
    return lat * r, r


def own_columns(qt, wh):
    head = lax.rem(lax.axis_index("frames"), 4)
    parts = []
    for s in range(3):
        x = qt[:, pl.ds(pl.multiple_of(s * 256 + (head // 2) * 128, 128), 128)].astype(F32)
        parts.append(jnp.where(lax.rem(head, 2) == 1, pltpu.roll(x, 64, 1), x))
    low = lanes((D, 128)) < 64
    wh[:, 0:128] = jnp.where(low, parts[0], pltpu.roll(parts[1], 64, 1)).astype(BF)
    wh[:, 128:256] = jnp.where(low, parts[2], 0.0).astype(BF)


def make_features(widths, spec, bw, feat, lat):
    bi = lax.axis_index("bands")
    start = jnp.int32(0)
    for j in range(NG):
        start = start + jnp.where(bi == 1, widths[j], 0)

    def one(k, start):
        w = widths[bi * NG + k]
        col = lax.broadcasted_iota(jnp.int32, (spec.shape[1], W), 0)
        lane = lanes((spec.shape[1], W))
        pick = jnp.logical_and(col - lane == 2 * start, lane < 2 * w)
        y = mm(spec[...], jnp.where(pick, 1.0, 0.0).astype(BF)).astype(BF)
        feat[k] = y
        lat[k] = mm(y, bw[rows_of(k, W), 0:D]).astype(BF)
        return start + w

    lax.fori_loop(0, NG, one, start)


def project(feat, bwk, wh, tables, q_s, k_s, kt_s, v_s, vt_s):
    def pre(j):
        rows = rows_of(j)
        f = feat[pl.ds(pl.multiple_of(j * 4, 4), 4)].reshape(BQ, W)
        n, _r = normed_rows(f, bwk[...])
        proj = mm(n.astype(BF), wh[...])
        co, si = angles_at(j, *tables)
        a = proj[:, :128]
        a = a * co + swap_halves(a) * si
        low = lanes(a.shape) < 64
        q_s[rows, :] = (a * (0.125 * LOG2E)).astype(BF)
        k = jnp.where(low, pltpu.roll(a, 64, 1), 0.0)
        k_s[rows, :] = k.astype(BF)
        kt_s[:, rows] = k.T[:64].astype(BF)
        v = jnp.where(low, proj[:, 128:], 1.0)
        v_s[rows, :] = v.astype(BF)
        vt_s[:, rows] = v.T.astype(BF)

    loop(0, NQ, pre)


def attend(blk, q_s, kt_s, v_s, e_s, s_s, ol, op):
    rows = rows_of(blk)
    q = q_s[rows, :][:, :64]
    top = jnp.full((BQ, 128), -jnp.inf, F32)
    for j in range(T // CF):
        cols = slice(j * CF, (j + 1) * CF)
        s = mm(q, kt_s[:, cols])
        s_s[:, cols] = s
        for i in range(CF // 128):
            top = jnp.maximum(top, s[:, 128 * i:128 * i + 128])
    top = jnp.max(top, axis=1, keepdims=True)
    res = jnp.zeros((BQ, 128), F32)
    for j in range(T // CF):
        cols = slice(j * CF, (j + 1) * CF)
        e = jnp.exp2(s_s[:, cols] - top).astype(BF)
        e_s[rows, cols] = e
        res = res + mm(e, v_s[cols, :])
    rl = 1.0 / res
    low = lanes(res.shape) < 64
    o = res * pltpu.roll(rl, 64, 1)
    ol[rows, :] = jnp.where(low, o, rl)
    o4 = o.reshape(BQ // HF, 2, 16, 128)
    low3 = lanes((BQ // HF, 16, 128)) < 64
    op[pl.ds(pl.multiple_of(blk * 8, 8), 8)] = jnp.where(low3, o4[:, 0], pltpu.roll(o4[:, 1], 64, 2)).astype(BF)


def attend_back(c, e_s, q_s, k_s, vt_s, ol, dop, t_s):
    rows = rows_of(c)
    x = dop[pl.ds(pl.multiple_of(c * 8, 8), 8)].astype(F32)
    do = jnp.concatenate([x[:, None], pltpu.roll(x, 64, 2)[:, None]], axis=1).reshape(BQ, 128)
    o = ol[rows, :]
    lane = lanes((BQ, 128))
    do = jnp.where(lane < 64, do * pltpu.roll(o, 64, 1), 0.0)
    delta = jnp.sum(do * o, axis=1, keepdims=True)
    hi = delta.astype(BF).astype(F32)
    aug = jnp.where(lane == 64, -hi, jnp.where(lane == 65, hi - delta, do)).astype(BF)
    do_t = do.T[:64].astype(BF)
    q_t = q_s[rows, :].astype(F32).T[:64].astype(BF)
    dq = jnp.zeros((BQ, 128), F32)
    for j in range(T // CB):
        cols = slice(j * CB, (j + 1) * CB)
        e = e_s[rows, cols]
        ds = (e.astype(F32) * mm(aug, vt_s[:, cols])).astype(BF)
        dq = dq + mm(ds, k_s[cols, :])
        t_s[0:64, cols] += mm(do_t, e)
        t_s[64:128, cols] += mm(q_t, ds)
    ol[rows, :] = dq * 0.125


def project_back(feat, bwk, wh, tables, dq_s, t_s, gb_s, gq_s):
    low = lanes((BQ, 128)) < 64
    gq_s[...] = jnp.zeros_like(gq_s)

    def post(j):
        rows = rows_of(j)
        tx = t_s[0:128, rows].T
        a = jnp.where(low, dq_s[rows, :], tx * math.log(2.0)).astype(BF).astype(F32)
        co, si = angles_at(j, *tables)
        a = a * co - swap_halves(a) * si
        dproj = jnp.concatenate([a, jnp.where(low, tx, 0.0)], axis=1).astype(BF)
        dn = mm(dproj, wh[...], NT).astype(BF).astype(F32)
        f = feat[pl.ds(pl.multiple_of(j * 4, 4), 4)].reshape(BQ, W)
        n, r = normed_rows(f, bwk[...])
        dlat = (r * (dn - n * jnp.mean(n * dn, axis=1, keepdims=True))).astype(BF)
        gb_s[...] += mm(f, dlat, TN)
        gq_s[...] += mm(n.astype(BF), dproj, TN)

    loop(0, NQ, post)


def band_layer(lat_all, lat_oth, cot_own, cot_oth, att, w_ot, w_qb, w_ob, cb, sb,
               lat_keep, lat_send, dsec_out, dop_out, wg_out, s_s, att_s, g_ot, g_qb, g_ob):
    bi = lax.axis_index("bands")
    own = pl.ds(pl.multiple_of(bi * 128, 128), 128)
    oth = pl.ds(pl.multiple_of((1 - bi) * 128, 128), 128)
    mine = pl.ds(pl.multiple_of(bi * HF, HF), HF)

    def lat_at(g):
        return pl.ds(pl.multiple_of(g * D, 128), D)

    def cot_at(g):
        return pl.ds(pl.multiple_of(4 * D + g * D, 128), D)

    def do_at(g):
        return pl.ds(pl.multiple_of(8 * D + g * 256, 128), 256)

    for x, at, where in ((lat_all[:, mine, :], lat_at, own), (lat_oth[...], lat_at, oth),
                         (cot_own[...], cot_at, own), (cot_oth[...], cot_at, oth)):
        x = x.astype(F32)
        for g in range(4):
            s_s[where, at(g)] = x[:, 8 * g:8 * g + 8, :].reshape(128, D)
    low = lanes((256, 128)) < 64

    def pair(a, b, p):
        if p == 0:
            return jnp.where(low, a, pltpu.roll(b, 64, 1))
        return jnp.where(low, pltpu.roll(a, 64, 1), b)

    for j in range(2):
        x0 = att[:, 2 * j].astype(F32)
        x1 = att[:, 2 * j + 1].astype(F32)
        for g in range(4):
            p, rr = g // 2, g % 2
            a = x0[:, 8 * rr:8 * rr + 8, :].reshape(256, 128)
            b = x1[:, 8 * rr:8 * rr + 8, :].reshape(256, 128)
            att_s[g, :, 128 * j:128 * j + 128] = pair(a, b, p).astype(BF)

    g_ot[...] = jnp.zeros_like(g_ot)
    g_qb[...] = jnp.zeros_like(g_qb)
    g_ob[...] = jnp.zeros_like(g_ob)

    def group(g):
        att_g = att_s[g]
        cot = s_s[:, cot_at(g)]
        cot_b = cot.astype(BF)
        sec = (s_s[:, lat_at(g)] + mm(att_g, w_ot[...])).astype(BF).astype(F32)
        r = lax.rsqrt(jnp.mean(sec * sec, axis=-1, keepdims=True) + EPS)
        n = sec * r
        nb = n.astype(BF)
        proj = mm(nb, w_qb[...])
        dbatt = mm(cot_b, w_ob[...], NT)
        co, si = cb[...], sb[...]
        row_t = lax.broadcasted_iota(jnp.int32, (256, 256), 0) % 8
        col_t = lax.broadcasted_iota(jnp.int32, (256, 256), 1) % 8
        same = row_t == col_t
        batts, dqs, dks, dvs = [], [], [], []
        for j in range(2):
            q = proj[:, 128 * j:128 * j + 128]
            k = proj[:, 256 + 128 * j:384 + 128 * j]
            v = proj[:, 512 + 128 * j:640 + 128 * j].astype(BF)
            q = ((q * co + swap_halves(q) * si) * 0.125).astype(BF)
            k = (k * co + swap_halves(k) * si).astype(BF)
            do = dbatt[:, 128 * j:128 * j + 128].astype(BF)
            outs = []
            for hh in range(2):
                part = low if hh == 0 else jnp.logical_not(low)
                zero = jnp.zeros((), BF)
                qm = jnp.where(part, q, zero)
                dm = jnp.where(part, do, zero)
                s = jnp.where(same, mm(qm, k, NT), -jnp.inf)
                e = jnp.exp(s - jnp.max(s, axis=1, keepdims=True))
                p = e * (1.0 / jnp.sum(e, axis=1, keepdims=True))
                pb = p.astype(BF)
                pf = pb.astype(F32)
                o = mm(pb, v)
                dp = mm(dm, v, NT)
                ds = (pf * (dp - jnp.sum(pf * dp, axis=1, keepdims=True))).astype(BF)
                outs.append((o, mm(ds, k), mm(ds, q, TN), mm(pb, do, TN)))
            batts.append(jnp.where(low, outs[0][0], outs[1][0]).astype(BF))
            dq = (jnp.where(low, outs[0][1], outs[1][1]) * 0.125).astype(BF).astype(F32)
            dk = jnp.where(low, outs[0][2], outs[1][2]).astype(BF).astype(F32)
            dqs.append((dq * co - swap_halves(dq) * si).astype(BF))
            dks.append((dk * co - swap_halves(dk) * si).astype(BF))
            dvs.append(jnp.where(low, outs[0][3], outs[1][3]).astype(BF))
        batt = jnp.concatenate(batts, axis=1)
        dproj = jnp.concatenate(dqs + dks + dvs, axis=1)
        s_s[:, lat_at(g)] = sec + mm(batt, w_ob[...])
        dn = mm(dproj, w_qb[...], NT).astype(BF).astype(F32)
        dsec = (cot + r * (dn - n * jnp.mean(n * dn, axis=1, keepdims=True))).astype(BF)
        s_s[:, cot_at(g)] = dsec.astype(F32)
        s_s[:, do_at(g)] = mm(dsec, w_ot[...], NT)
        g_ob[...] += mm(batt, cot_b, TN)
        g_qb[...] += mm(nb, dproj, TN)
        g_ot[...] += mm(att_g, dsec, TN)

    loop(0, 4, group)

    for j in range(2):
        for hh in range(2):
            parts = []
            for rr in range(2):
                a = s_s[:, do_at(rr)][:, 128 * j:128 * j + 128]
                b = s_s[:, do_at(2 + rr)][:, 128 * j:128 * j + 128]
                parts.append(pair(a, b, hh).reshape(NB, 8, 128))
            dop_out[:, 2 * j + hh] = jnp.concatenate(parts, axis=1).astype(BF)

    def rest():
        dsec_out[...] = jnp.concatenate(
            [s_s[:, cot_at(g)].reshape(NB, 8, D) for g in range(4)], axis=1
        ).astype(BF)
        for ref, where in ((lat_keep, own), (lat_send, oth)):
            ref[...] = jnp.concatenate(
                [s_s[where, lat_at(g)].reshape(NG, 8, D) for g in range(4)], axis=1
            ).astype(BF)
        wg_out[0:16] = g_ot[...].reshape(16, 16, D).astype(BF)
        wg_out[16:64] = jnp.concatenate(
            [g_qb[:, :D].reshape(48, 8, D), g_qb[:, D:].reshape(48, 8, D)], axis=1
        ).astype(BF)
        wg_out[64:80] = g_ob[...].reshape(16, 16, D).astype(BF)

    return rest


def kernel(widths, spec, bw, qt, w_ot, w_qb, w_ob, cot, cc, sc, cr, sr, cb, sb,
           latent, out, wg_r, gsum, wsum,
           e_s, s_s, feat_own, feat, lat_all, lat_oth, cot_own, cot_oth, wh, q_s, k_s, kt_s, v_s, vt_s,
           ol, op, att, att_s, g_ot, g_qb, g_ob, lat_keep, lat_send, dsec, dop, wg, dop_r, dsec_r,
           bwk, gb_s, gq_s, gband, gq, quad, part, gq_r, send, recv, local):
    fi, bi = here()
    me = fi * 2 + bi
    slot = bi * NF + fi
    head = lax.rem(fi, 4)
    tables = (cc, sc, cr, sr)
    mine = pl.ds(pl.multiple_of(bi * HF, HF), HF)
    other = pl.ds(pl.multiple_of((1 - bi) * HF, HF), HF)

    bw_at = e_s.at[pl.ds(0, NG * W), pl.ds(0, D)]
    bw_copy = pltpu.make_async_copy(bw, bw_at, local.at[0])
    bw_copy.start()
    cot_copy = pltpu.make_async_copy(cot.at[:, mine, :], cot_own, local.at[1])
    cot_copy.start()

    barrier = pltpu.get_barrier_semaphore()

    def greet(d):
        t = lax.rem(me + d, ND)
        pl.semaphore_signal(barrier, inc=1, device_id=(t // 2, lax.rem(t, 2)), device_id_type=MESH)

    loop(1, ND, greet)

    own_columns(qt, wh)
    bw_copy.wait()
    make_features(widths, spec, e_s, feat_own, lat_all)
    bwk[...] = e_s[rows_of(fi // 4, W), 0:D]
    pl.semaphore_wait(barrier, ND - 1)

    pltpu.make_async_copy(feat_own.at[fi // 4], feat.at[fi], recv.at[0]).start()

    def give_features(d):
        t = lax.rem(fi + d, NF)
        copy_to(feat_own.at[t // 4], feat.at[fi], send.at[0], recv.at[0], t, bi)

    loop(1, NF, give_features)
    copy_to(lat_all.at[:, other, :], lat_oth, send.at[1], recv.at[1], fi, 1 - bi)
    copy_to(cot.at[:, other, :], cot_oth, send.at[2], recv.at[2], fi, 1 - bi)

    wait_bytes(feat, recv.at[0])
    project(feat, bwk, wh, tables, q_s, k_s, kt_s, v_s, vt_s)

    def forward(c):
        blk = lax.rem(c + fi // 4, NQ)
        attend(blk, q_s, kt_s, v_s, e_s, s_s, ol, op)

        def give(u):
            d = blk * 8 + u
            copy_out(op.at[d], att.at[slot], send.at[3], recv.at[3], d // 2, lax.rem(d, 2))

        loop(0, 8, give)

    loop(0, NQ, forward)

    wait_bytes(lat_oth, recv.at[1])
    wait_bytes(cot_oth, recv.at[2])
    cot_copy.wait()
    wait_bytes(att, recv.at[3])
    rest = band_layer(
        lat_all, lat_oth, cot_own, cot_oth, att.reshape(NB, 4, 16, 128), w_ot, w_qb, w_ob, cb, sb,
        lat_keep, lat_send, dsec, dop.reshape(NB, 4, 16, 128), wg, s_s, att_s, g_ot, g_qb, g_ob)

    pltpu.make_async_copy(dop.at[slot], dop_r.at[me], recv.at[4]).start()

    def give_back(d):
        t = lax.rem(slot + d, ND)
        copy_to(dop.at[t], dop_r.at[me], send.at[4], recv.at[4], lax.rem(t, NF), t // NF)

    loop(1, ND, give_back)
    rest()

    quarter = fi // 16
    place = lax.rem(fi, 16) * 2 + bi

    def give_second(k):
        copy_out(dsec.at[k], dsec_r.at[place], send.at[5], recv.at[5],
                 lax.rem(k, NG) * 4 + quarter, k // NG)

    loop(0, NB, give_second)
    copy_to(lat_send, latent.at[:, mine, :], send.at[7], recv.at[7], fi, 1 - bi)
    lat_copy = pltpu.make_async_copy(lat_keep, latent.at[:, mine, :], local.at[1])
    lat_copy.start()

    def give_weights(d):
        copy_out(wg.at[d - 48], wg_r.at[rows_of(me, 16)], send.at[6], recv.at[6], d // 2, lax.rem(d, 2))

    loop(48, ND, give_weights)

    s_s[0:128, :] = jnp.zeros((128, T), F32)
    wait_bytes(dop_r, recv.at[4])
    loop(0, NQ, lambda c: attend_back(c, e_s, q_s, k_s, vt_s, ol, dop_r, s_s))

    wait_bytes(dsec_r, recv.at[5])
    f = feat[pl.ds(pl.multiple_of(head * 16, 16), 16)].reshape(1024, W)
    gb_s[...] = mm(f, dsec_r[...].reshape(1024, D), TN)
    project_back(feat, bwk, wh, tables, ol, s_s, gb_s, gq_s)

    gband[...] = gb_s[...].reshape(4, 32, D).astype(BF)
    base = fi - head
    pltpu.make_async_copy(gband.at[head], quad.at[head], recv.at[8]).start()
    for d in range(1, 4):
        t = lax.rem(head + d, 4)
        copy_to(gband.at[t], quad.at[head], send.at[8], recv.at[8], base + t, bi)
    g = gq_s[...]
    gq[...] = jnp.concatenate(
        [g[:, :128].reshape(48, 8, 128), g[:, 128:].reshape(48, 8, 128)], axis=1
    ).astype(BF)
    loop(0, 48, lambda d: copy_out(gq.at[d], gq_r.at[me], send.at[9], recv.at[9], d // 2, lax.rem(d, 2)))

    wait_bytes(quad, recv.at[8])
    part[...] = jnp.sum(quad[...].astype(F32), axis=0).astype(BF)
    pltpu.make_async_copy(part, out.at[fi], recv.at[10]).start()

    def give_band(d):
        copy_to(part, out.at[fi], send.at[10], recv.at[10], lax.rem(fi + d, NF), bi)

    loop(1, NF, give_band)

    @pl.when(me < 48)
    def _():
        wsum[...] = jnp.zeros_like(wsum)
        wait_bytes(gq_r, recv.at[9])
        x = gq_r[...].reshape(NG, 4, 2, 16, 128)
        gsum[...] = jnp.sum(x.astype(F32), axis=(0, 2))

    @pl.when(me >= 48)
    def _():
        gsum[...] = jnp.zeros_like(gsum)
        wait_bytes(wg_r, recv.at[6])
        at = e_s.at[pl.ds(0, ND * 16), pl.ds(0, D)]
        fetch = pltpu.make_async_copy(wg_r, at, local.at[2])
        fetch.start()
        fetch.wait()
        wsum[...] = jnp.sum(e_s[0:ND * 16, 0:D].astype(F32).reshape(ND, 16, D), axis=0)

    wait_bytes(latent.at[:, other, :], recv.at[7])
    lat_copy.wait()
    wait_bytes(out, recv.at[10])
    wait_bytes(feat.at[pl.ds(0, NF - 1)], send.at[0])
    wait_bytes(lat_oth, send.at[1])
    wait_bytes(cot_oth, send.at[2])
    wait_bytes(op.at[pl.ds(0, ND - 1)], send.at[3])
    wait_bytes(dop.at[pl.ds(0, ND - 1)], send.at[4])
    wait_bytes(dsec.at[pl.ds(0, NB - 1)], send.at[5])
    wait_bytes(lat_send, send.at[7])
    wait_bytes(gband.at[pl.ds(0, 3)], send.at[8])
    wait_bytes(gq.at[pl.ds(0, 47)], send.at[9])
    wait_bytes(wg.at[pl.ds(0, 79)], send.at[6])
    wait_bytes(out.at[pl.ds(0, NF - 1)], send.at[10])

    @pl.when(head != quarter)
    def _():
        wait_bytes(dsec.at[0], send.at[5])

    @pl.when(me >= 48)
    def _():
        wait_bytes(gq.at[0], send.at[9])

    @pl.when(me < 48)
    def _():
        wait_bytes(wg.at[0], send.at[6])


VM = pl.BlockSpec(memory_space=pltpu.VMEM)
SM = pl.BlockSpec(memory_space=pltpu.SMEM)
ANY = pl.BlockSpec(memory_space=pl.ANY)


def struct(shape, dtype):
    return jax.ShapeDtypeStruct(shape, dtype)


def shards(spectrum, band_widths, band_weight, qkv_time, out_time, qkv_band, out_band, cotangent):
    fi, bi = here()
    me = fi * 2 + bi
    tables = rotary_tables(np.arange(NQ) * BQ) + rotary_tables(np.arange(BQ)) + rotary_tables(np.arange(256) // 8)
    tables = tuple(jnp.asarray(x) for x in tables)

    def vm(shape, dtype=BF):
        return pltpu.VMEM(shape, dtype)

    latent, out, _wg_r, gsum, wsum = pl.pallas_call(
        kernel,
        out_shape=[struct((NG, FB, D), BF), struct((NF, 32, D), BF), struct((ND * 16, D), BF),
                   struct((4, 16, 128), F32), struct((16, D), F32)],
        in_specs=[SM, VM, ANY, VM, VM, VM, VM, ANY] + [VM] * 6,
        out_specs=[ANY, ANY, ANY, VM, VM],
        scratch_shapes=[
            vm((T, T)), vm((BQ, T), F32), vm((NG, FB, W)), vm((NF, FB, W)), vm((NG, FB, D)),
            vm((NG, HF, D)), vm((NG, HF, D)), vm((NG, HF, D)), vm((D, 256)),
            vm((T, 128)), vm((T, 128)), vm((64, T)), vm((T, 128)), vm((128, T)),
            vm((T, 128), F32), vm((ND, 16, 128)), vm((ND, 16, 128)), vm((4, 256, 256)),
            vm((256, D), F32), vm((D, 768), F32), vm((256, D), F32),
            vm((NG, HF, D)), vm((NG, HF, D)), vm((NB, HF, D)), vm((ND, 16, 128)), vm((80, 16, D)),
            vm((ND, 16, 128)), vm((NB, HF, D)),
            vm((W, D)), vm((W, D), F32), vm((D, 256), F32), vm((4, 32, D)), vm((48, 16, 128)),
            vm((4, 32, D)), vm((32, D)), vm((ND, 16, 128)),
            pltpu.SemaphoreType.DMA((11,)), pltpu.SemaphoreType.DMA((11,)), pltpu.SemaphoreType.DMA((3,)),
        ],
        compiler_params=pltpu.CompilerParams(
            collective_id=1, has_side_effects=True, vmem_limit_bytes=VMEM_LIMIT
        ),
    )(band_widths, spectrum[0], band_weight.reshape(NG * W, D), qkv_time, out_time, qkv_band, out_band,
      cotangent[0], *tables)

    band_grad = out.reshape(NG, W, D).astype(F32)
    gt = jnp.stack([gsum[:, :8, :64], gsum[:, :8, 64:], gsum[:, 8:, :64]])
    share_t = gt.transpose(2, 0, 1, 3).reshape(-1)
    share_q = wsum.reshape(2, 8, D).transpose(1, 0, 2).reshape(-1)
    share = jnp.where(me < 48, share_t, jnp.where((me >= 64) & (me < 112), share_q, wsum.reshape(-1)))
    return (latent[None], band_grad, share)


def solution(mesh):
    placed = (
        P(None, "frames", None),
        P(),
        P("bands", None, None),
        P(),
        P(),
        P(),
        P(),
        P(None, "bands", "frames", None),
    )
    return jax.shard_map(
        shards,
        mesh=mesh,
        in_specs=placed,
        out_specs=(
            P(None, "bands", "frames", None),
            P("bands", None, None),
            P(("frames", "bands")),
        ),
        check_vma=False,
    )
```

time: 1510 us -> 215 us (0.14)
  the two profiles are of different devices: /device:TPU:1 before, /device:TPU:57 now
where the time goes in v2:
time: 215 us
  Pallas kernels  207 us (96%)
  other arithmetic  4.1 us (2%)
  local copies, waits for them, and re-layouts  3.37 us (2%)
    pallas_call x1, Pallas kernels, shards(): pl.pallas_call(kernel, out_shape=[struct((NG, FB, D), BF), struct((NF, 32...  207 us

profile of v2, /device:TPU:57, one launch (start us, length us, event | category | flops | bytes accessed | tf_op | source)
XLA Modules:
  0.0 214.7 jit_solution(17965008814998261264)
XLA Ops:
  0.6 206.6 %shard_map.157 = (bf16[16,64,384]{2,1,0:T(8,128)(2,1)}, bf16[64,32,384]{2,1,0:T(8,128)(2,1)}, bf16[2048,384]{1,0:T(8,128)(2,1)}, f32[4,16,128]{2,1,0:T(8,128)}, f32[16,384]{1,0:T(8,128)}) custom-call(s32[32]{0:T(128)} %widths.1, bf16[64,1280]{1,0:T(8,128)(2,1)} %bitcast.24, bf16[2048,384]{1,0:T(8,128)(2,1)} %bitcast.20, bf16[384,768]{1,0:T(8,128)(2,1)} %qt.1, ...), custom_call_target="tpu_custom_call" | custom-call | tf_op jit(solution)/shard_map/pallas_call | solution.py:539
  207.2 0.8 copy.20
  208.0 0.7 reshape.28
  208.7 0.9 slice_bitcast_fusion.2
  209.6 0.1 reshape.25
  209.7 0.6 select_select_fusion
  210.3 0.0 copy-start
  210.3 3.5 %bitcast_convert_fusion = f32[16,128,384]{2,1,0:T(8,128)} fusion(bf16[16,128,384]{2,1,0:T(8,128)(2,1)} %bitcast.21), kind=kLoop, calls=%fused_computation | loop fusion | flops 786432 | bytes 4718592 | tf_op jit(solution)/shard_map/convert_element_type | solution.py:563
  213.8 0.0 copy-done
  213.8 0.9 copy.22
  (3 shorter events, 0.0 us)
Async XLA Ops:
  210.3 3.5 %copy-start = (bf16[16,64,384]{2,1,0:T(8,128)(2,1)S(1)}, bf16[16,64,384]{2,1,0:T(8,128)(2,1)}, u32[]{:S(2)}) copy-start(bf16[16,64,384]{2,1,0:T(8,128)(2,1)} %get-tuple-element.7) | copy-start | bytes 2359300

commit v3 on v2

--- a/solution.py
+++ b/solution.py
@@ -21,6 +21,8 @@
 W = 128
 BQ = 256
 NQ = T // BQ
+BP = 512
+NP = T // BP
 CF = 512
 CB = 1024
 LOG2E = math.log2(math.e)
@@ -137,10 +139,14 @@
     lax.fori_loop(0, NG, one, start)
 
 
-def project(feat, bwk, wh, tables, q_s, k_s, kt_s, v_s, vt_s):
-    def pre(j):
-        rows = rows_of(j)
-        f = feat[pl.ds(pl.multiple_of(j * 4, 4), 4)].reshape(BQ, W)
+def project(feat, arrived, bwk, wh, tables, q_s, k_s, kt_s, v_s, vt_s):
+    fi, _ = here()
+
+    def pre(i):
+        j = lax.rem(fi // 8 + 2 * NP - 1 - i, NP)
+        rows = rows_of(j, BP)
+        wait_bytes(feat.at[rows_of(j, 8)], arrived.at[j])
+        f = feat[rows_of(j, 8)].reshape(BP, W)
         n, _r = normed_rows(f, bwk[...])
         proj = mm(n.astype(BF), wh[...])
         co, si = angles_at(j, *tables)
@@ -155,7 +161,7 @@
         v_s[rows, :] = v.astype(BF)
         vt_s[:, rows] = v.T.astype(BF)
 
-    loop(0, NQ, pre)
+    loop(0, NP, pre)
 
 
 def attend(blk, q_s, kt_s, v_s, e_s, s_s, ol, op):
@@ -207,29 +213,29 @@
     ol[rows, :] = dq * 0.125
 
 
-def project_back(feat, bwk, wh, tables, dq_s, t_s, gb_s, gq_s):
-    low = lanes((BQ, 128)) < 64
-    gq_s[...] = jnp.zeros_like(gq_s)
+def project_back(feat, bwk, wh, tables, dq_s, t_s, gb_s, dproj_s, n_s):
+    low = lanes((BP, 128)) < 64
 
     def post(j):
-        rows = rows_of(j)
+        rows = rows_of(j, BP)
         tx = t_s[0:128, rows].T
         a = jnp.where(low, dq_s[rows, :], tx * math.log(2.0)).astype(BF).astype(F32)
         co, si = angles_at(j, *tables)
         a = a * co - swap_halves(a) * si
         dproj = jnp.concatenate([a, jnp.where(low, tx, 0.0)], axis=1).astype(BF)
         dn = mm(dproj, wh[...], NT).astype(BF).astype(F32)
-        f = feat[pl.ds(pl.multiple_of(j * 4, 4), 4)].reshape(BQ, W)
+        f = feat[rows_of(j, 8)].reshape(BP, W)
         n, r = normed_rows(f, bwk[...])
         dlat = (r * (dn - n * jnp.mean(n * dn, axis=1, keepdims=True))).astype(BF)
         gb_s[...] += mm(f, dlat, TN)
-        gq_s[...] += mm(n.astype(BF), dproj, TN)
-
-    loop(0, NQ, post)
+        dproj_s[rows, :] = dproj
+        n_s[rows, :] = n.astype(BF)
+
+    loop(0, NP, post)
 
 
 def band_layer(lat_all, lat_oth, cot_own, cot_oth, att, w_ot, w_qb, w_ob, cb, sb,
-               lat_keep, lat_send, dsec_out, dop_out, wg_out, s_s, att_s, g_ot, g_qb, g_ob):
+               lat_keep, lat_send, dsec_out, dop_out, wg_out, s_s, att_s, g_ot, g_qb, g_ob, wait_att):
     bi = lax.axis_index("bands")
     own = pl.ds(pl.multiple_of(bi * 128, 128), 128)
     oth = pl.ds(pl.multiple_of((1 - bi) * 128, 128), 128)
@@ -249,7 +255,11 @@
         x = x.astype(F32)
         for g in range(4):
             s_s[where, at(g)] = x[:, 8 * g:8 * g + 8, :].reshape(128, D)
+    g_ot[...] = jnp.zeros_like(g_ot)
+    g_qb[...] = jnp.zeros_like(g_qb)
+    g_ob[...] = jnp.zeros_like(g_ob)
     low = lanes((256, 128)) < 64
+    wait_att()
 
     def pair(a, b, p):
         if p == 0:
@@ -264,10 +274,6 @@
             a = x0[:, 8 * rr:8 * rr + 8, :].reshape(256, 128)
             b = x1[:, 8 * rr:8 * rr + 8, :].reshape(256, 128)
             att_s[g, :, 128 * j:128 * j + 128] = pair(a, b, p).astype(BF)
-
-    g_ot[...] = jnp.zeros_like(g_ot)
-    g_qb[...] = jnp.zeros_like(g_qb)
-    g_ob[...] = jnp.zeros_like(g_ob)
 
     def group(g):
         att_g = att_s[g]
@@ -351,11 +357,13 @@
     return rest
 
 
-def kernel(widths, spec, bw, qt, w_ot, w_qb, w_ob, cot, cc, sc, cr, sr, cb, sb,
-           latent, out, wg_r, gsum, wsum,
+def kernel(widths, spec_h, bw, qt_h, w_ot_h, w_qb_h, w_ob_h, cot, cc_h, sc_h, cr_h, sr_h, cb_h, sb_h,
+           latent, out, wg_r, share,
+           spec, qt, w_ot, w_qb, w_ob, cc, sc, cr, sr, cb, sb,
            e_s, s_s, feat_own, feat, lat_all, lat_oth, cot_own, cot_oth, wh, q_s, k_s, kt_s, v_s, vt_s,
            ol, op, att, att_s, g_ot, g_qb, g_ob, lat_keep, lat_send, dsec, dop, wg, dop_r, dsec_r,
-           bwk, gb_s, gq_s, gband, gq, quad, part, gq_r, send, recv, local):
+           bwk, gb_s, gq_s, gband, gq, quad, part, gq_r, send, recv, local,
+           feat_in, dop_in, out_in, staged):
     fi, bi = here()
     me = fi * 2 + bi
     slot = bi * NF + fi
@@ -364,12 +372,6 @@
     mine = pl.ds(pl.multiple_of(bi * HF, HF), HF)
     other = pl.ds(pl.multiple_of((1 - bi) * HF, HF), HF)
 
-    bw_at = e_s.at[pl.ds(0, NG * W), pl.ds(0, D)]
-    bw_copy = pltpu.make_async_copy(bw, bw_at, local.at[0])
-    bw_copy.start()
-    cot_copy = pltpu.make_async_copy(cot.at[:, mine, :], cot_own, local.at[1])
-    cot_copy.start()
-
     barrier = pltpu.get_barrier_semaphore()
 
     def greet(d):
@@ -378,24 +380,33 @@
 
     loop(1, ND, greet)
 
+    bw_at = e_s.at[pl.ds(0, NG * W), pl.ds(0, D)]
+    first = ((bw, bw_at), (spec_h, spec), (qt_h, qt))
+    later = ((cc_h, cc), (sc_h, sc), (cr_h, cr), (sr_h, sr), (w_ot_h, w_ot), (w_qb_h, w_qb), (w_ob_h, w_ob),
+             (cb_h, cb), (sb_h, sb), (cot.at[:, mine, :], cot_own))
+    copies = [pltpu.make_async_copy(x, y, staged.at[i]) for i, (x, y) in enumerate(first + later)]
+    for c in copies:
+        c.start()
+    for c in copies[:len(first)]:
+        c.wait()
     own_columns(qt, wh)
-    bw_copy.wait()
     make_features(widths, spec, e_s, feat_own, lat_all)
     bwk[...] = e_s[rows_of(fi // 4, W), 0:D]
+    for c in copies[len(first):]:
+        c.wait()
     pl.semaphore_wait(barrier, ND - 1)
 
-    pltpu.make_async_copy(feat_own.at[fi // 4], feat.at[fi], recv.at[0]).start()
+    pltpu.make_async_copy(feat_own.at[fi // 4], feat.at[fi], feat_in.at[fi // 8]).start()
 
     def give_features(d):
         t = lax.rem(fi + d, NF)
-        copy_to(feat_own.at[t // 4], feat.at[fi], send.at[0], recv.at[0], t, bi)
+        copy_to(feat_own.at[t // 4], feat.at[fi], send.at[0], feat_in.at[fi // 8], t, bi)
 
     loop(1, NF, give_features)
     copy_to(lat_all.at[:, other, :], lat_oth, send.at[1], recv.at[1], fi, 1 - bi)
     copy_to(cot.at[:, other, :], cot_oth, send.at[2], recv.at[2], fi, 1 - bi)
 
-    wait_bytes(feat, recv.at[0])
-    project(feat, bwk, wh, tables, q_s, k_s, kt_s, v_s, vt_s)
+    project(feat, feat_in, bwk, wh, tables, q_s, k_s, kt_s, v_s, vt_s)
 
     def forward(c):
         blk = lax.rem(c + fi // 4, NQ)
@@ -411,19 +422,21 @@
 
     wait_bytes(lat_oth, recv.at[1])
     wait_bytes(cot_oth, recv.at[2])
-    cot_copy.wait()
-    wait_bytes(att, recv.at[3])
     rest = band_layer(
         lat_all, lat_oth, cot_own, cot_oth, att.reshape(NB, 4, 16, 128), w_ot, w_qb, w_ob, cb, sb,
-        lat_keep, lat_send, dsec, dop.reshape(NB, 4, 16, 128), wg, s_s, att_s, g_ot, g_qb, g_ob)
-
-    pltpu.make_async_copy(dop.at[slot], dop_r.at[me], recv.at[4]).start()
+        lat_keep, lat_send, dsec, dop.reshape(NB, 4, 16, 128), wg, s_s, att_s, g_ot, g_qb, g_ob,
+        lambda: wait_bytes(att, recv.at[3]))
+
+    group = fi // 4
+    pltpu.make_async_copy(dop.at[slot], dop_r.at[me], dop_in.at[group]).start()
+    copy_to(dop.at[(1 - bi) * NF + fi], dop_r.at[me], send.at[4], dop_in.at[group], fi, 1 - bi)
 
     def give_back(d):
-        t = lax.rem(slot + d, ND)
-        copy_to(dop.at[t], dop_r.at[me], send.at[4], recv.at[4], lax.rem(t, NF), t // NF)
-
-    loop(1, ND, give_back)
+        f = lax.rem(fi + d, NF)
+        copy_to(dop.at[f], dop_r.at[me], send.at[4], dop_in.at[group], f, 0)
+        copy_to(dop.at[NF + f], dop_r.at[me], send.at[4], dop_in.at[group], f, 1)
+
+    loop(1, NF, give_back)
     rest()
 
     quarter = fi // 16
@@ -444,13 +457,20 @@
     loop(48, ND, give_weights)
 
     s_s[0:128, :] = jnp.zeros((128, T), F32)
-    wait_bytes(dop_r, recv.at[4])
-    loop(0, NQ, lambda c: attend_back(c, e_s, q_s, k_s, vt_s, ol, dop_r, s_s))
+
+    def backward(i):
+        c = lax.rem(group + 2 * NQ - 1 - i, NQ)
+        wait_bytes(dop_r.at[rows_of(c, 8)], dop_in.at[c])
+        attend_back(c, e_s, q_s, k_s, vt_s, ol, dop_r, s_s)
+
+    loop(0, NQ, backward)
 
     wait_bytes(dsec_r, recv.at[5])
-    f = feat[pl.ds(pl.multiple_of(head * 16, 16), 16)].reshape(1024, W)
+    f = feat[rows_of(head, 16)].reshape(1024, W)
     gb_s[...] = mm(f, dsec_r[...].reshape(1024, D), TN)
-    project_back(feat, bwk, wh, tables, ol, s_s, gb_s, gq_s)
+    dproj_s = e_s.at[:, pl.ds(0, 256)]
+    n_s = e_s.at[:, pl.ds(256, D)]
+    project_back(feat, bwk, wh, tables, ol, s_s, gb_s, dproj_s, n_s)
 
     gband[...] = gb_s[...].reshape(4, 32, D).astype(BF)
     base = fi - head
@@ -458,42 +478,79 @@
     for d in range(1, 4):
         t = lax.rem(head + d, 4)
         copy_to(gband.at[t], quad.at[head], send.at[8], recv.at[8], base + t, bi)
+
+    gq_s[...] = jnp.zeros_like(gq_s)
+
+    def weight(j):
+        rows = rows_of(j, 1024)
+        gq_s[...] += mm(n_s[rows, :], dproj_s[rows, :], TN)
+
+    loop(0, 4, weight)
+
+    chip, core = fi // 2, lax.rem(fi, 2)
+    mate = fi + 1 - 2 * core
+    wait_bytes(quad, recv.at[8])
+    part[...] = jnp.sum(quad[...].astype(F32), axis=0).astype(BF)
+    pltpu.make_async_copy(part, out.at[chip, core], out_in.at[chip // 4]).start()
+
+    def give_band(d):
+        copy_to(part, out.at[chip, core], send.at[10], out_in.at[chip // 4],
+                lax.rem(chip + d, 32) * 2 + core, bi)
+
+    loop(1, 32, give_band)
+
     g = gq_s[...]
     gq[...] = jnp.concatenate(
         [g[:, :128].reshape(48, 8, 128), g[:, 128:].reshape(48, 8, 128)], axis=1
     ).astype(BF)
     loop(0, 48, lambda d: copy_out(gq.at[d], gq_r.at[me], send.at[9], recv.at[9], d // 2, lax.rem(d, 2)))
 
-    wait_bytes(quad, recv.at[8])
-    part[...] = jnp.sum(quad[...].astype(F32), axis=0).astype(BF)
-    pltpu.make_async_copy(part, out.at[fi], recv.at[10]).start()
-
-    def give_band(d):
-        copy_to(part, out.at[fi], send.at[10], recv.at[10], lax.rem(fi + d, NF), bi)
-
-    loop(1, NF, give_band)
+    def pass_on(i):
+        j = lax.rem(chip // 4 + 15 - i, 8)
+        block = out.at[rows_of(j, 4), core]
+        wait_bytes(block, out_in.at[j])
+        copy_to(block, block, send.at[0], recv.at[10], mate, bi)
+
+    low8 = lanes((8, 128)) < 64
+
+    wait_bytes(feat.at[pl.ds(0, NF - 1)], send.at[0])
+    loop(0, 8, pass_on)
 
     @pl.when(me < 48)
     def _():
-        wsum[...] = jnp.zeros_like(wsum)
         wait_bytes(gq_r, recv.at[9])
-        x = gq_r[...].reshape(NG, 4, 2, 16, 128)
-        gsum[...] = jnp.sum(x.astype(F32), axis=(0, 2))
+        x = jnp.sum(gq_r[...].reshape(NG, 4, 2, 16, 128).astype(F32), axis=(0, 2))
+        for j in range(2):
+            a, b = x[2 * j], x[2 * j + 1]
+            share[pl.ds(j, 8, stride=6), :] = jnp.where(low8, a[:8], pltpu.roll(b[:8], 64, 1))
+            share[pl.ds(2 + j, 8, stride=6), :] = jnp.where(low8, pltpu.roll(a[:8], 64, 1), b[:8])
+            share[pl.ds(4 + j, 8, stride=6), :] = jnp.where(low8, a[8:], pltpu.roll(b[8:], 64, 1))
 
     @pl.when(me >= 48)
     def _():
-        gsum[...] = jnp.zeros_like(gsum)
         wait_bytes(wg_r, recv.at[6])
-        at = e_s.at[pl.ds(0, ND * 16), pl.ds(0, D)]
+        at = e_s.at[pl.ds(0, ND * 16), pl.ds(1024, D)]
         fetch = pltpu.make_async_copy(wg_r, at, local.at[2])
         fetch.start()
         fetch.wait()
-        wsum[...] = jnp.sum(e_s[0:ND * 16, 0:D].astype(F32).reshape(ND, 16, D), axis=0)
+        x = jnp.sum(e_s[0:ND * 16, 1024:1024 + D].astype(F32).reshape(ND, 16, D), axis=0)
+        wide = jnp.logical_and(me >= 64, me < 112)
+
+        @pl.when(wide)
+        def _():
+            for j in range(3):
+                share[pl.ds(j, 8, stride=6), :] = x[:8, 128 * j:128 * j + 128]
+                share[pl.ds(3 + j, 8, stride=6), :] = x[8:, 128 * j:128 * j + 128]
+
+        @pl.when(jnp.logical_not(wide))
+        def _():
+            for j in range(3):
+                share[pl.ds(j, 16, stride=3), :] = x[:, 128 * j:128 * j + 128]
 
     wait_bytes(latent.at[:, other, :], recv.at[7])
     lat_copy.wait()
-    wait_bytes(out, recv.at[10])
-    wait_bytes(feat.at[pl.ds(0, NF - 1)], send.at[0])
+    wait_bytes(out.at[:, 1 - core], recv.at[10])
+    wait_bytes(out.at[:, core], send.at[0])
     wait_bytes(lat_oth, send.at[1])
     wait_bytes(cot_oth, send.at[2])
     wait_bytes(op.at[pl.ds(0, ND - 1)], send.at[3])
@@ -503,7 +560,7 @@
     wait_bytes(gband.at[pl.ds(0, 3)], send.at[8])
     wait_bytes(gq.at[pl.ds(0, 47)], send.at[9])
     wait_bytes(wg.at[pl.ds(0, 79)], send.at[6])
-    wait_bytes(out.at[pl.ds(0, NF - 1)], send.at[10])
+    wait_bytes(out.at[pl.ds(0, 31), core], send.at[10])
 
     @pl.when(head != quarter)
     def _():
@@ -528,21 +585,22 @@
 
 
 def shards(spectrum, band_widths, band_weight, qkv_time, out_time, qkv_band, out_band, cotangent):
-    fi, bi = here()
-    me = fi * 2 + bi
-    tables = rotary_tables(np.arange(NQ) * BQ) + rotary_tables(np.arange(BQ)) + rotary_tables(np.arange(256) // 8)
+    tables = rotary_tables(np.arange(NP) * BP) + rotary_tables(np.arange(BP)) + rotary_tables(np.arange(256) // 8)
     tables = tuple(jnp.asarray(x) for x in tables)
 
     def vm(shape, dtype=BF):
         return pltpu.VMEM(shape, dtype)
 
-    latent, out, _wg_r, gsum, wsum = pl.pallas_call(
+    latent, out, _wg_r, share = pl.pallas_call(
         kernel,
-        out_shape=[struct((NG, FB, D), BF), struct((NF, 32, D), BF), struct((ND * 16, D), BF),
-                   struct((4, 16, 128), F32), struct((16, D), F32)],
-        in_specs=[SM, VM, ANY, VM, VM, VM, VM, ANY] + [VM] * 6,
-        out_specs=[ANY, ANY, ANY, VM, VM],
+        out_shape=[struct((NG, FB, D), BF), struct((32, 2, 32, D), BF), struct((ND * 16, D), BF),
+                   struct((48, 128), F32)],
+        in_specs=[SM] + [ANY] * 13,
+        out_specs=[ANY, ANY, ANY, VM],
         scratch_shapes=[
+            vm((FB, 1280)), vm((D, 768)), vm((256, D)), vm((D, 768)), vm((256, D)),
+            vm((NP, 128), F32), vm((NP, 128), F32), vm((BP, 128), F32), vm((BP, 128), F32),
+            vm((256, 128), F32), vm((256, 128), F32),
             vm((T, T)), vm((BQ, T), F32), vm((NG, FB, W)), vm((NF, FB, W)), vm((NG, FB, D)),
             vm((NG, HF, D)), vm((NG, HF, D)), vm((NG, HF, D)), vm((D, 256)),
             vm((T, 128)), vm((T, 128)), vm((64, T)), vm((T, 128)), vm((128, T)),
@@ -553,6 +611,8 @@
             vm((W, D)), vm((W, D), F32), vm((D, 256), F32), vm((4, 32, D)), vm((48, 16, 128)),
             vm((4, 32, D)), vm((32, D)), vm((ND, 16, 128)),
             pltpu.SemaphoreType.DMA((11,)), pltpu.SemaphoreType.DMA((11,)), pltpu.SemaphoreType.DMA((3,)),
+            pltpu.SemaphoreType.DMA((NP,)), pltpu.SemaphoreType.DMA((NQ,)), pltpu.SemaphoreType.DMA((8,)),
+            pltpu.SemaphoreType.DMA((13,)),
         ],
         compiler_params=pltpu.CompilerParams(
             collective_id=1, has_side_effects=True, vmem_limit_bytes=VMEM_LIMIT
@@ -561,11 +621,7 @@
       cotangent[0], *tables)
 
     band_grad = out.reshape(NG, W, D).astype(F32)
-    gt = jnp.stack([gsum[:, :8, :64], gsum[:, :8, 64:], gsum[:, 8:, :64]])
-    share_t = gt.transpose(2, 0, 1, 3).reshape(-1)
-    share_q = wsum.reshape(2, 8, D).transpose(1, 0, 2).reshape(-1)
-    share = jnp.where(me < 48, share_t, jnp.where((me >= 64) & (me < 112), share_q, wsum.reshape(-1)))
-    return (latent[None], band_grad, share)
+    return (latent[None], band_grad, share.reshape(-1))
 
 
 def solution(mesh):

time: 215 us -> 177 us (0.82)
  the two profiles are of different devices: /device:TPU:57 before, /device:TPU:1 now
where the time goes in v3:
time: 177 us
  Pallas kernels  172 us (97%)
  other arithmetic  3.48 us (2%)
    pallas_call x1, Pallas kernels, shards(): pl.pallas_call(kernel, out_shape=[struct((NG, FB, D), BF), struct((32, 2,...  172 us

profile of v3, /device:TPU:1, one launch (start us, length us, event | category | flops | bytes accessed | tf_op | source)
XLA Modules:
  0.0 177.3 jit_solution(17764675000323818680)
XLA Ops:
  0.6 171.7 %shard_map.157 = (bf16[16,64,384]{2,1,0:T(8,128)(2,1)}, bf16[32,2,32,384]{3,2,1,0:T(8,128)(2,1)}, bf16[2048,384]{1,0:T(8,128)(2,1)}, f32[48,128]{1,0:T(8,128)}) custom-call(s32[32]{0:T(128)} %widths.1, bf16[64,1280]{1,0:T(8,128)(2,1)} %bitcast.11, bf16[2048,384]{1,0:T(8,128)(2,1)} %bitcast.7, bf16[384,768]{1,0:T(8,128)(2,1)} %qt_h.1, ...), custom_call_target="tpu_custom_call" | custom-call | tf_op jit(solution)/shard_map/pallas_call | solution.py:594
  172.3 0.0 copy-start
  172.3 3.5 %convert.1 = f32[16,128,384]{2,1,0:T(8,128)} convert(bf16[16,128,384]{2,1,0:T(8,128)(2,1)} %bitcast.8) | non-fusion elementwise | flops 786432 | bytes 4718592 | tf_op jit(solution)/shard_map/convert_element_type | solution.py:623
  175.8 0.0 copy-done
  175.8 0.0 copy-start.1
  175.8 0.9 copy.19
  176.7 0.0 copy-done.1
  176.7 0.6 copy.20
Async XLA Ops:
  172.3 3.5 %copy-start = (bf16[16,64,384]{2,1,0:T(8,128)(2,1)S(1)}, bf16[16,64,384]{2,1,0:T(8,128)(2,1)}, u32[]{:S(2)}) copy-start(bf16[16,64,384]{2,1,0:T(8,128)(2,1)} %get-tuple-element.6) | copy-start | bytes 2359300
  175.8 0.9 copy-start.1

commit v4 on v3

--- a/solution.py
+++ b/solution.py
@@ -139,7 +139,7 @@
     lax.fori_loop(0, NG, one, start)
 
 
-def project(feat, arrived, bwk, wh, tables, q_s, k_s, kt_s, v_s, vt_s):
+def project(feat, arrived, bwk, wh, tables, q_s, k_s, kt_s, v_s, vt_s, midway):
     fi, _ = here()
 
     def pre(i):
@@ -160,6 +160,7 @@
         v = jnp.where(low, proj[:, 128:], 1.0)
         v_s[rows, :] = v.astype(BF)
         vt_s[:, rows] = v.T.astype(BF)
+        pl.when(i == 5)(midway)
 
     loop(0, NP, pre)
 
@@ -358,12 +359,13 @@
 
 
 def kernel(widths, spec_h, bw, qt_h, w_ot_h, w_qb_h, w_ob_h, cot, cc_h, sc_h, cr_h, sr_h, cb_h, sb_h,
-           latent, out, wg_r, share,
+           latent, out, share,
            spec, qt, w_ot, w_qb, w_ob, cc, sc, cr, sr, cb, sb,
            e_s, s_s, feat_own, feat, lat_all, lat_oth, cot_own, cot_oth, wh, q_s, k_s, kt_s, v_s, vt_s,
            ol, op, att, att_s, g_ot, g_qb, g_ob, lat_keep, lat_send, dsec, dop, wg, dop_r, dsec_r,
            bwk, gb_s, gq_s, gband, gq, quad, part, gq_r, send, recv, local,
-           feat_in, dop_in, out_in, staged):
+           feat_in, dop_in, out_in, staged,
+           wg_p, wg_s, wg_r, rows_in, group_in):
     fi, bi = here()
     me = fi * 2 + bi
     slot = bi * NF + fi
@@ -374,11 +376,16 @@
 
     barrier = pltpu.get_barrier_semaphore()
 
+    row, col = fi // 8, lax.rem(fi, 8)
+
     def greet(d):
-        t = lax.rem(me + d, ND)
-        pl.semaphore_signal(barrier, inc=1, device_id=(t // 2, lax.rem(t, 2)), device_id_type=MESH)
-
-    loop(1, ND, greet)
+        in_row = row * 8 + lax.rem(col + d, 8)
+        in_col = lax.rem(row + d, 8) * 8 + col
+        pl.semaphore_signal(barrier, inc=1, device_id=(in_row, bi), device_id_type=MESH)
+        pl.semaphore_signal(barrier, inc=1, device_id=(in_col, bi), device_id_type=MESH)
+
+    loop(1, 8, greet)
+    pl.semaphore_signal(barrier, inc=1, device_id=(fi, 1 - bi), device_id_type=MESH)
 
     bw_at = e_s.at[pl.ds(0, NG * W), pl.ds(0, D)]
     first = ((bw, bw_at), (spec_h, spec), (qt_h, qt))
@@ -394,7 +401,15 @@
     bwk[...] = e_s[rows_of(fi // 4, W), 0:D]
     for c in copies[len(first):]:
         c.wait()
-    pl.semaphore_wait(barrier, ND - 1)
+    pl.semaphore_wait(barrier, 15)
+
+    def greet_again(d):
+        in_col = lax.rem(row + d, 8) * 8 + col
+        pl.semaphore_signal(rows_in, inc=1, device_id=(in_col, bi), device_id_type=MESH)
+
+    loop(1, 8, greet_again)
+    pl.semaphore_wait(rows_in, 7)
+    pl.semaphore_signal(group_in, inc=1, device_id=(fi, 1 - bi), device_id_type=MESH)
 
     pltpu.make_async_copy(feat_own.at[fi // 4], feat.at[fi], feat_in.at[fi // 8]).start()
 
@@ -403,10 +418,13 @@
         copy_to(feat_own.at[t // 4], feat.at[fi], send.at[0], feat_in.at[fi // 8], t, bi)
 
     loop(1, NF, give_features)
-    copy_to(lat_all.at[:, other, :], lat_oth, send.at[1], recv.at[1], fi, 1 - bi)
-    copy_to(cot.at[:, other, :], cot_oth, send.at[2], recv.at[2], fi, 1 - bi)
-
-    project(feat, feat_in, bwk, wh, tables, q_s, k_s, kt_s, v_s, vt_s)
+
+    def give_halves():
+        copy_to(cot.at[:, other, :], cot_oth, send.at[2], recv.at[2], fi, 1 - bi)
+        copy_to(lat_all.at[:, other, :], lat_oth, send.at[1], recv.at[1], fi, 1 - bi)
+
+    project(feat, feat_in, bwk, wh, tables, q_s, k_s, kt_s, v_s, vt_s, give_halves)
+    pl.semaphore_wait(group_in, 1)
 
     def forward(c):
         blk = lax.rem(c + fi // 4, NQ)
@@ -442,19 +460,35 @@
     quarter = fi // 16
     place = lax.rem(fi, 16) * 2 + bi
 
-    def give_second(k):
-        copy_out(dsec.at[k], dsec_r.at[place], send.at[5], recv.at[5],
-                 lax.rem(k, NG) * 4 + quarter, k // NG)
-
-    loop(0, NB, give_second)
-    copy_to(lat_send, latent.at[:, mine, :], send.at[7], recv.at[7], fi, 1 - bi)
-    lat_copy = pltpu.make_async_copy(lat_keep, latent.at[:, mine, :], local.at[1])
-    lat_copy.start()
-
-    def give_weights(d):
-        copy_out(wg.at[d - 48], wg_r.at[rows_of(me, 16)], send.at[6], recv.at[6], d // 2, lax.rem(d, 2))
-
-    loop(48, ND, give_weights)
+    def give_second():
+        def one(k):
+            copy_out(dsec.at[k], dsec_r.at[place], send.at[5], recv.at[5],
+                     lax.rem(k, NG) * 4 + quarter, k // NG)
+
+        loop(0, NB, one)
+
+    def give_latent():
+        copy_to(lat_send, latent.at[:, mine, :], send.at[7], recv.at[7], fi, 1 - bi)
+        pltpu.make_async_copy(lat_keep, latent.at[:, mine, :], local.at[1]).start()
+
+    def give_weights():
+        pltpu.make_async_copy(wg.at[rows_of(col, 10)], wg_p.at[col], recv.at[6]).start()
+
+        def one(d):
+            t = lax.rem(col + d, 8)
+            copy_to(wg.at[rows_of(t, 10)], wg_p.at[col], send.at[6], recv.at[6], row * 8 + t, bi)
+
+        loop(1, 8, one)
+
+    def give_sums():
+        wait_bytes(wg_p, recv.at[6])
+        wg_s[...] = jnp.sum(wg_p[...].astype(F32), axis=0).astype(BF)
+
+        def one(u):
+            d = 48 + col * 10 + u
+            copy_out(wg_s.at[u], wg_r.at[row * 2 + bi], send.at[11], recv.at[11], d // 2, lax.rem(d, 2))
+
+        loop(0, 10, one)
 
     s_s[0:128, :] = jnp.zeros((128, T), F32)
 
@@ -462,6 +496,10 @@
         c = lax.rem(group + 2 * NQ - 1 - i, NQ)
         wait_bytes(dop_r.at[rows_of(c, 8)], dop_in.at[c])
         attend_back(c, e_s, q_s, k_s, vt_s, ol, dop_r, s_s)
+        pl.when(i == 3)(give_second)
+        pl.when(i == 5)(give_weights)
+        pl.when(i == 7)(give_latent)
+        pl.when(i == 13)(give_sums)
 
     loop(0, NQ, backward)
 
@@ -528,12 +566,8 @@
 
     @pl.when(me >= 48)
     def _():
-        wait_bytes(wg_r, recv.at[6])
-        at = e_s.at[pl.ds(0, ND * 16), pl.ds(1024, D)]
-        fetch = pltpu.make_async_copy(wg_r, at, local.at[2])
-        fetch.start()
-        fetch.wait()
-        x = jnp.sum(e_s[0:ND * 16, 1024:1024 + D].astype(F32).reshape(ND, 16, D), axis=0)
+        wait_bytes(wg_r, recv.at[11])
+        x = jnp.sum(wg_r[...].astype(F32), axis=0)
         wide = jnp.logical_and(me >= 64, me < 112)
 
         @pl.when(wide)
@@ -548,7 +582,7 @@
                 share[pl.ds(j, 16, stride=3), :] = x[:, 128 * j:128 * j + 128]
 
     wait_bytes(latent.at[:, other, :], recv.at[7])
-    lat_copy.wait()
+    pltpu.make_async_copy(lat_keep, latent.at[:, mine, :], local.at[1]).wait()
     wait_bytes(out.at[:, 1 - core], recv.at[10])
     wait_bytes(out.at[:, core], send.at[0])
     wait_bytes(lat_oth, send.at[1])
@@ -559,7 +593,8 @@
     wait_bytes(lat_send, send.at[7])
     wait_bytes(gband.at[pl.ds(0, 3)], send.at[8])
     wait_bytes(gq.at[pl.ds(0, 47)], send.at[9])
-    wait_bytes(wg.at[pl.ds(0, 79)], send.at[6])
+    wait_bytes(wg.at[pl.ds(0, 70)], send.at[6])
+    wait_bytes(wg_s.at[pl.ds(0, 9)], send.at[11])
     wait_bytes(out.at[pl.ds(0, 31), core], send.at[10])
 
     @pl.when(head != quarter)
@@ -570,9 +605,9 @@
     def _():
         wait_bytes(gq.at[0], send.at[9])
 
-    @pl.when(me < 48)
+    @pl.when(jnp.logical_or(me < 48, (me - 48) // 10 != col))
     def _():
-        wait_bytes(wg.at[0], send.at[6])
+        wait_bytes(wg_s.at[0], send.at[11])
 
 
 VM = pl.BlockSpec(memory_space=pltpu.VMEM)
@@ -591,12 +626,11 @@
     def vm(shape, dtype=BF):
         return pltpu.VMEM(shape, dtype)
 
-    latent, out, _wg_r, share = pl.pallas_call(
+    latent, out, share = pl.pallas_call(
         kernel,
-        out_shape=[struct((NG, FB, D), BF), struct((32, 2, 32, D), BF), struct((ND * 16, D), BF),
-                   struct((48, 128), F32)],
+        out_shape=[struct((NG, FB, D), BF), struct((32, 2, 32, D), BF), struct((48, 128), F32)],
         in_specs=[SM] + [ANY] * 13,
-        out_specs=[ANY, ANY, ANY, VM],
+        out_specs=[ANY, ANY, VM],
         scratch_shapes=[
             vm((FB, 1280)), vm((D, 768)), vm((256, D)), vm((D, 768)), vm((256, D)),
             vm((NP, 128), F32), vm((NP, 128), F32), vm((BP, 128), F32), vm((BP, 128), F32),
@@ -610,9 +644,11 @@
             vm((ND, 16, 128)), vm((NB, HF, D)),
             vm((W, D)), vm((W, D), F32), vm((D, 256), F32), vm((4, 32, D)), vm((48, 16, 128)),
             vm((4, 32, D)), vm((32, D)), vm((ND, 16, 128)),
-            pltpu.SemaphoreType.DMA((11,)), pltpu.SemaphoreType.DMA((11,)), pltpu.SemaphoreType.DMA((3,)),
+            pltpu.SemaphoreType.DMA((12,)), pltpu.SemaphoreType.DMA((12,)), pltpu.SemaphoreType.DMA((3,)),
             pltpu.SemaphoreType.DMA((NP,)), pltpu.SemaphoreType.DMA((NQ,)), pltpu.SemaphoreType.DMA((8,)),
             pltpu.SemaphoreType.DMA((13,)),
+            vm((8, 10, 16, D)), vm((10, 16, D)), vm((16, 16, D)),
+            pltpu.SemaphoreType.REGULAR, pltpu.SemaphoreType.REGULAR,
         ],
         compiler_params=pltpu.CompilerParams(
             collective_id=1, has_side_effects=True, vmem_limit_bytes=VMEM_LIMIT

time: 177 us -> 170 us (0.960)
  Pallas kernels: 172 us -> 164 us
    pallas_call x1, Pallas kernels: 172 us -> 164 us  [shards(): pl.pallas_call(kernel, out_shape=[struct((NG, FB, D), BF), struct((32, 2,...]
where the time goes in v4:
time: 170 us
  Pallas kernels  164 us (96%)
  other arithmetic  3.48 us (2%)
    pallas_call x1, Pallas kernels, shards(): pl.pallas_call(kernel, out_shape=[struct((NG, FB, D), BF), struct((32, 2,...  164 us
    convert_element_type x1, other arithmetic, shards(): band_grad = out.reshape(NG, W, D).astype(F32)  3.48 us

profile of v4, /device:TPU:1, one launch (start us, length us, event | category | flops | bytes accessed | tf_op | source)
XLA Modules:
  0.0 170.0 jit_solution(4259152239783787947)
XLA Ops:
  0.6 164.4 %shard_map.157 = (bf16[16,64,384]{2,1,0:T(8,128)(2,1)}, bf16[32,2,32,384]{3,2,1,0:T(8,128)(2,1)}, f32[48,128]{1,0:T(8,128)}) custom-call(s32[32]{0:T(128)} %widths.1, bf16[64,1280]{1,0:T(8,128)(2,1)} %bitcast.11, bf16[2048,384]{1,0:T(8,128)(2,1)} %bitcast.7, bf16[384,768]{1,0:T(8,128)(2,1)} %qt_h.1, bf16[256,384]{1,0:T(8,128)(2,1)} %w_ot_h.1, ...), custom_call_target="tpu_custom_call" | custom-call | tf_op jit(solution)/shard_map/pallas_call | solution.py:629
  165.0 0.0 copy-start
  165.0 3.5 %convert.1 = f32[16,128,384]{2,1,0:T(8,128)} convert(bf16[16,128,384]{2,1,0:T(8,128)(2,1)} %bitcast.8) | non-fusion elementwise | flops 786432 | bytes 4718592 | tf_op jit(solution)/shard_map/convert_element_type | solution.py:659
  168.5 0.0 copy-done
  168.5 0.0 copy-start.1
  168.5 0.9 copy.19
  169.4 0.0 copy-done.1
  169.4 0.6 copy.20
Async XLA Ops:
  165.0 3.5 %copy-start = (bf16[16,64,384]{2,1,0:T(8,128)(2,1)S(1)}, bf16[16,64,384]{2,1,0:T(8,128)(2,1)}, u32[]{:S(2)}) copy-start(bf16[16,64,384]{2,1,0:T(8,128)(2,1)} %get-tuple-element.6) | copy-start | bytes 2359300
  168.5 0.9 copy-start.1

commit v5 on v4

--- a/solution.py
+++ b/solution.py
@@ -126,12 +126,21 @@
     for j in range(NG):
         start = start + jnp.where(bi == 1, widths[j], 0)
 
+    lane = lanes((256, W))
+    diff = lax.broadcasted_iota(jnp.int32, (256, W), 0) - lane
+
     def one(k, start):
         w = widths[bi * NG + k]
-        col = lax.broadcasted_iota(jnp.int32, (spec.shape[1], W), 0)
-        lane = lanes((spec.shape[1], W))
-        pick = jnp.logical_and(col - lane == 2 * start, lane < 2 * w)
-        y = mm(spec[...], jnp.where(pick, 1.0, 0.0).astype(BF)).astype(BF)
+        blk = (2 * start) // 128
+        a = spec[:, 0:128]
+        b = spec[:, 128:256]
+        last = spec.shape[1] // 128 - 1
+        for n in range(1, last + 1):
+            a = jnp.where(blk == n, spec[:, 128 * n:128 * n + 128], a)
+        for n in range(2, last + 1):
+            b = jnp.where(blk == n - 1, spec[:, 128 * n:128 * n + 128], b)
+        pick = jnp.logical_and(diff == 2 * start - 128 * blk, lane < 2 * w)
+        y = mm(jnp.concatenate([a, b], axis=1), jnp.where(pick, 1.0, 0.0).astype(BF)).astype(BF)
         feat[k] = y
         lat[k] = mm(y, bw[rows_of(k, W), 0:D]).astype(BF)
         return start + w
@@ -139,13 +148,9 @@
     lax.fori_loop(0, NG, one, start)
 
 
-def project(feat, arrived, bwk, wh, tables, q_s, k_s, kt_s, v_s, vt_s, midway):
-    fi, _ = here()
-
-    def pre(i):
-        j = lax.rem(fi // 8 + 2 * NP - 1 - i, NP)
+def project(feat, step, bwk, wh, tables, q_s, k_s, kt_s, v_s, vt_s):
+    def pre(j):
         rows = rows_of(j, BP)
-        wait_bytes(feat.at[rows_of(j, 8)], arrived.at[j])
         f = feat[rows_of(j, 8)].reshape(BP, W)
         n, _r = normed_rows(f, bwk[...])
         proj = mm(n.astype(BF), wh[...])
@@ -160,9 +165,12 @@
         v = jnp.where(low, proj[:, 128:], 1.0)
         v_s[rows, :] = v.astype(BF)
         vt_s[:, rows] = v.T.astype(BF)
-        pl.when(i == 5)(midway)
-
-    loop(0, NP, pre)
+
+    def quarter(i):
+        at = step(i)
+        loop(0, 2, lambda u: pre(2 * at + u))
+
+    loop(0, 4, quarter)
 
 
 def attend(blk, q_s, kt_s, v_s, e_s, s_s, ol, op):
@@ -362,7 +370,7 @@
            latent, out, share,
            spec, qt, w_ot, w_qb, w_ob, cc, sc, cr, sr, cb, sb,
            e_s, s_s, feat_own, feat, lat_all, lat_oth, cot_own, cot_oth, wh, q_s, k_s, kt_s, v_s, vt_s,
-           ol, op, att, att_s, g_ot, g_qb, g_ob, lat_keep, lat_send, dsec, dop, wg, dop_r, dsec_r,
+           ol, op, att, att_s, g_ot, g_qb, g_ob, dsec, dop, wg, dop_r, dsec_r,
            bwk, gb_s, gq_s, gband, gq, quad, part, gq_r, send, recv, local,
            feat_in, dop_in, out_in, staged,
            wg_p, wg_s, wg_r, rows_in, group_in):
@@ -411,39 +419,83 @@
     pl.semaphore_wait(rows_in, 7)
     pl.semaphore_signal(group_in, inc=1, device_id=(fi, 1 - bi), device_id_type=MESH)
 
-    pltpu.make_async_copy(feat_own.at[fi // 4], feat.at[fi], feat_in.at[fi // 8]).start()
+    quarter = fi // 16
 
     def give_features(d):
-        t = lax.rem(fi + d, NF)
-        copy_to(feat_own.at[t // 4], feat.at[fi], send.at[0], feat_in.at[fi // 8], t, bi)
-
-    loop(1, NF, give_features)
+        k = lax.rem(fi + d, NG)
+        copy_out(feat_own.at[k], feat.at[fi], send.at[0], feat_in.at[0, lax.rem(fi, 16) // 4], 4 * k + quarter, bi)
+
+    loop(0, NG, give_features)
+    mate = fi + 1 - 2 * lax.rem(fi, 2)
+    near = fi + 2 - 4 * lax.rem(fi // 2, 2)
 
     def give_halves():
         copy_to(cot.at[:, other, :], cot_oth, send.at[2], recv.at[2], fi, 1 - bi)
         copy_to(lat_all.at[:, other, :], lat_oth, send.at[1], recv.at[1], fi, 1 - bi)
 
-    project(feat, feat_in, bwk, wh, tables, q_s, k_s, kt_s, v_s, vt_s, give_halves)
+    def part_of(quarter, q):
+        return feat.at[pl.ds(pl.multiple_of(quarter * 16 + q * 4, 4), 4)]
+
+    def spread(q):
+        block = part_of(head, q)
+        wait_bytes(block, feat_in.at[0, q])
+        copy_to(block, block, send.at[12], feat_in.at[1, q], mate, bi)
+        copy_to(block, block, send.at[12], feat_in.at[2, q], near, bi)
+
+    loop(0, 4, spread)
+
+    def step(i):
+        at = 2 * lax.rem(head // 2 + i // 2, 2) + lax.rem(head + i, 2)
+
+        @pl.when(i == 1)
+        def _():
+            give_halves()
+
+        @pl.when(i == 2)
+        def _():
+            def forward_on(q):
+                block = part_of(at, q)
+                wait_bytes(block, feat_in.at[2, q])
+                copy_to(block, block, send.at[12], feat_in.at[3, q], mate, bi)
+
+            loop(0, 4, forward_on)
+
+        @pl.when(lax.rem(i, 2) == 1)
+        def _():
+            loop(0, 4, lambda q: wait_bytes(part_of(at, q), feat_in.at[i, q]))
+
+        return at
+
+    project(feat, step, bwk, wh, tables, q_s, k_s, kt_s, v_s, vt_s)
     pl.semaphore_wait(group_in, 1)
 
+    def give_block(blk):
+        for u in range(8):
+            d = blk * 8 + u
+            self_here = d == me
+            copy_to(op.at[d], att.at[jnp.where(self_here, (1 - bi) * NF + fi, slot)], send.at[3], recv.at[3],
+                    jnp.where(self_here, fi, d // 2), jnp.where(self_here, 1 - bi, lax.rem(d, 2)))
+
+    first_blk = fi // 4
+    attend(first_blk, q_s, kt_s, v_s, e_s, s_s, ol, op)
+
     def forward(c):
-        blk = lax.rem(c + fi // 4, NQ)
-        attend(blk, q_s, kt_s, v_s, e_s, s_s, ol, op)
-
-        def give(u):
-            d = blk * 8 + u
-            copy_out(op.at[d], att.at[slot], send.at[3], recv.at[3], d // 2, lax.rem(d, 2))
-
-        loop(0, 8, give)
-
-    loop(0, NQ, forward)
+        give_block(lax.rem(c + first_blk + NQ - 1, NQ))
+        attend(lax.rem(c + first_blk, NQ), q_s, kt_s, v_s, e_s, s_s, ol, op)
+
+    loop(1, NQ, forward)
+    give_block(lax.rem(first_blk + NQ - 1, NQ))
+
+    def wait_att():
+        wait_bytes(att, recv.at[3])
+        att[slot] = op[me]
 
     wait_bytes(lat_oth, recv.at[1])
     wait_bytes(cot_oth, recv.at[2])
     rest = band_layer(
         lat_all, lat_oth, cot_own, cot_oth, att.reshape(NB, 4, 16, 128), w_ot, w_qb, w_ob, cb, sb,
-        lat_keep, lat_send, dsec, dop.reshape(NB, 4, 16, 128), wg, s_s, att_s, g_ot, g_qb, g_ob,
-        lambda: wait_bytes(att, recv.at[3]))
+        cot_own, cot_oth, dsec, dop.reshape(NB, 4, 16, 128), wg, s_s, att_s, g_ot, g_qb, g_ob,
+        wait_att)
 
     group = fi // 4
     pltpu.make_async_copy(dop.at[slot], dop_r.at[me], dop_in.at[group]).start()
@@ -457,7 +509,6 @@
     loop(1, NF, give_back)
     rest()
 
-    quarter = fi // 16
     place = lax.rem(fi, 16) * 2 + bi
 
     def give_second():
@@ -468,8 +519,8 @@
         loop(0, NB, one)
 
     def give_latent():
-        copy_to(lat_send, latent.at[:, mine, :], send.at[7], recv.at[7], fi, 1 - bi)
-        pltpu.make_async_copy(lat_keep, latent.at[:, mine, :], local.at[1]).start()
+        copy_to(cot_oth, latent.at[:, mine, :], send.at[7], recv.at[7], fi, 1 - bi)
+        pltpu.make_async_copy(cot_own, latent.at[:, mine, :], local.at[1]).start()
 
     def give_weights():
         pltpu.make_async_copy(wg.at[rows_of(col, 10)], wg_p.at[col], recv.at[6]).start()
@@ -526,7 +577,6 @@
     loop(0, 4, weight)
 
     chip, core = fi // 2, lax.rem(fi, 2)
-    mate = fi + 1 - 2 * core
     wait_bytes(quad, recv.at[8])
     part[...] = jnp.sum(quad[...].astype(F32), axis=0).astype(BF)
     pltpu.make_async_copy(part, out.at[chip, core], out_in.at[chip // 4]).start()
@@ -547,11 +597,10 @@
         j = lax.rem(chip // 4 + 15 - i, 8)
         block = out.at[rows_of(j, 4), core]
         wait_bytes(block, out_in.at[j])
-        copy_to(block, block, send.at[0], recv.at[10], mate, bi)
+        copy_to(block, block, send.at[13], recv.at[10], mate, bi)
 
     low8 = lanes((8, 128)) < 64
 
-    wait_bytes(feat.at[pl.ds(0, NF - 1)], send.at[0])
     loop(0, 8, pass_on)
 
     @pl.when(me < 48)
@@ -582,15 +631,17 @@
                 share[pl.ds(j, 16, stride=3), :] = x[:, 128 * j:128 * j + 128]
 
     wait_bytes(latent.at[:, other, :], recv.at[7])
-    pltpu.make_async_copy(lat_keep, latent.at[:, mine, :], local.at[1]).wait()
+    pltpu.make_async_copy(cot_own, latent.at[:, mine, :], local.at[1]).wait()
     wait_bytes(out.at[:, 1 - core], recv.at[10])
-    wait_bytes(out.at[:, core], send.at[0])
+    wait_bytes(out.at[:, core], send.at[13])
+    wait_bytes(feat.at[pl.ds(0, NG - 1)], send.at[0])
+    wait_bytes(feat.at[pl.ds(0, 48)], send.at[12])
     wait_bytes(lat_oth, send.at[1])
     wait_bytes(cot_oth, send.at[2])
-    wait_bytes(op.at[pl.ds(0, ND - 1)], send.at[3])
+    wait_bytes(op, send.at[3])
     wait_bytes(dop.at[pl.ds(0, ND - 1)], send.at[4])
     wait_bytes(dsec.at[pl.ds(0, NB - 1)], send.at[5])
-    wait_bytes(lat_send, send.at[7])
+    wait_bytes(cot_oth, send.at[7])
     wait_bytes(gband.at[pl.ds(0, 3)], send.at[8])
     wait_bytes(gq.at[pl.ds(0, 47)], send.at[9])
     wait_bytes(wg.at[pl.ds(0, 70)], send.at[6])
@@ -599,6 +650,7 @@
 
     @pl.when(head != quarter)
     def _():
+        wait_bytes(feat.at[0], send.at[0])
         wait_bytes(dsec.at[0], send.at[5])
 
     @pl.when(me >= 48)
@@ -640,12 +692,12 @@
             vm((T, 128)), vm((T, 128)), vm((64, T)), vm((T, 128)), vm((128, T)),
             vm((T, 128), F32), vm((ND, 16, 128)), vm((ND, 16, 128)), vm((4, 256, 256)),
             vm((256, D), F32), vm((D, 768), F32), vm((256, D), F32),
-            vm((NG, HF, D)), vm((NG, HF, D)), vm((NB, HF, D)), vm((ND, 16, 128)), vm((80, 16, D)),
+            vm((NB, HF, D)), vm((ND, 16, 128)), vm((80, 16, D)),
             vm((ND, 16, 128)), vm((NB, HF, D)),
             vm((W, D)), vm((W, D), F32), vm((D, 256), F32), vm((4, 32, D)), vm((48, 16, 128)),
             vm((4, 32, D)), vm((32, D)), vm((ND, 16, 128)),
-            pltpu.SemaphoreType.DMA((12,)), pltpu.SemaphoreType.DMA((12,)), pltpu.SemaphoreType.DMA((3,)),
-            pltpu.SemaphoreType.DMA((NP,)), pltpu.SemaphoreType.DMA((NQ,)), pltpu.SemaphoreType.DMA((8,)),
+            pltpu.SemaphoreType.DMA((14,)), pltpu.SemaphoreType.DMA((12,)), pltpu.SemaphoreType.DMA((3,)),
+            pltpu.SemaphoreType.DMA((4, 4)), pltpu.SemaphoreType.DMA((NQ,)), pltpu.SemaphoreType.DMA((8,)),
             pltpu.SemaphoreType.DMA((13,)),
             vm((8, 10, 16, D)), vm((10, 16, D)), vm((16, 16, D)),
             pltpu.SemaphoreType.REGULAR, pltpu.SemaphoreType.REGULAR,

time: 170 us -> 168 us (0.988)
  Pallas kernels: 164 us -> 162 us
    pallas_call x1, Pallas kernels: 164 us -> 162 us  [shards(): pl.pallas_call(kernel, out_shape=[struct((NG, FB, D), BF), struct((32, 2,...]
where the time goes in v5:
time: 168 us
  Pallas kernels  162 us (96%)
  other arithmetic  3.48 us (2%)
    pallas_call x1, Pallas kernels, shards(): pl.pallas_call(kernel, out_shape=[struct((NG, FB, D), BF), struct((32, 2,...  162 us
    convert_element_type x1, other arithmetic, shards(): band_grad = out.reshape(NG, W, D).astype(F32)  3.48 us

profile of v5, /device:TPU:1, one launch (start us, length us, event | category | flops | bytes accessed | tf_op | source)
XLA Modules:
  0.0 167.7 jit_solution(8713891453146550780)
XLA Ops:
  0.6 162.0 %shard_map.157 = (bf16[16,64,384]{2,1,0:T(8,128)(2,1)}, bf16[32,2,32,384]{3,2,1,0:T(8,128)(2,1)}, f32[48,128]{1,0:T(8,128)}) custom-call(s32[32]{0:T(128)} %widths.1, bf16[64,1280]{1,0:T(8,128)(2,1)} %bitcast.11, bf16[2048,384]{1,0:T(8,128)(2,1)} %bitcast.7, bf16[384,768]{1,0:T(8,128)(2,1)} %qt_h.1, bf16[256,384]{1,0:T(8,128)(2,1)} %w_ot_h.1, ...), custom_call_target="tpu_custom_call" | custom-call | tf_op jit(solution)/shard_map/pallas_call | solution.py:681
  162.7 0.0 copy-start
  162.7 3.5 %convert.1 = f32[16,128,384]{2,1,0:T(8,128)} convert(bf16[16,128,384]{2,1,0:T(8,128)(2,1)} %bitcast.8) | non-fusion elementwise | flops 786432 | bytes 4718592 | tf_op jit(solution)/shard_map/convert_element_type | solution.py:711
  166.2 0.0 copy-done
  166.2 0.0 copy-start.1
  166.2 0.9 copy.19
  167.0 0.0 copy-done.1
  167.0 0.6 copy.20
Async XLA Ops:
  162.7 3.5 %copy-start = (bf16[16,64,384]{2,1,0:T(8,128)(2,1)S(1)}, bf16[16,64,384]{2,1,0:T(8,128)(2,1)}, u32[]{:S(2)}) copy-start(bf16[16,64,384]{2,1,0:T(8,128)(2,1)} %get-tuple-element.6) | copy-start | bytes 2359300
  166.2 0.9 copy-start.1

commit v6 on v5

--- a/solution.py
+++ b/solution.py
@@ -402,6 +402,13 @@
     copies = [pltpu.make_async_copy(x, y, staged.at[i]) for i, (x, y) in enumerate(first + later)]
     for c in copies:
         c.start()
+    pl.semaphore_wait(barrier, 15)
+
+    def greet_again(d):
+        in_col = lax.rem(row + d, 8) * 8 + col
+        pl.semaphore_signal(rows_in, inc=1, device_id=(in_col, bi), device_id_type=MESH)
+
+    loop(1, 8, greet_again)
     for c in copies[:len(first)]:
         c.wait()
     own_columns(qt, wh)
@@ -409,13 +416,6 @@
     bwk[...] = e_s[rows_of(fi // 4, W), 0:D]
     for c in copies[len(first):]:
         c.wait()
-    pl.semaphore_wait(barrier, 15)
-
-    def greet_again(d):
-        in_col = lax.rem(row + d, 8) * 8 + col
-        pl.semaphore_signal(rows_in, inc=1, device_id=(in_col, bi), device_id_type=MESH)
-
-    loop(1, 8, greet_again)
     pl.semaphore_wait(rows_in, 7)
     pl.semaphore_signal(group_in, inc=1, device_id=(fi, 1 - bi), device_id_type=MESH)
 
@@ -506,7 +506,11 @@
         copy_to(dop.at[f], dop_r.at[me], send.at[4], dop_in.at[group], f, 0)
         copy_to(dop.at[NF + f], dop_r.at[me], send.at[4], dop_in.at[group], f, 1)
 
-    loop(1, NF, give_back)
+    def give_some(n):
+        for u in range(7):
+            give_back(1 + 7 * n + u)
+
+    loop(0, 9, give_some)
     rest()
 
     place = lax.rem(fi, 16) * 2 + bi

time: 168 us -> 166 us (0.988)
  Pallas kernels: 162 us -> 160 us
    pallas_call x1, Pallas kernels: 162 us -> 160 us  [shards(): pl.pallas_call(kernel, out_shape=[struct((NG, FB, D), BF), struct((32, 2,...]
where the time goes in v6:
time: 166 us
  Pallas kernels  160 us (96%)
  other arithmetic  3.48 us (2%)
    pallas_call x1, Pallas kernels, shards(): pl.pallas_call(kernel, out_shape=[struct((NG, FB, D), BF), struct((32, 2,...  160 us
    convert_element_type x1, other arithmetic, shards(): band_grad = out.reshape(NG, W, D).astype(F32)  3.48 us

profile of v6, /device:TPU:1, one launch (start us, length us, event | category | flops | bytes accessed | tf_op | source)
XLA Modules:
  0.0 165.7 jit_solution(2131414571700762126)
XLA Ops:
  0.6 160.1 %shard_map.157 = (bf16[16,64,384]{2,1,0:T(8,128)(2,1)}, bf16[32,2,32,384]{3,2,1,0:T(8,128)(2,1)}, f32[48,128]{1,0:T(8,128)}) custom-call(s32[32]{0:T(128)} %widths.1, bf16[64,1280]{1,0:T(8,128)(2,1)} %bitcast.11, bf16[2048,384]{1,0:T(8,128)(2,1)} %bitcast.7, bf16[384,768]{1,0:T(8,128)(2,1)} %qt_h.1, bf16[256,384]{1,0:T(8,128)(2,1)} %w_ot_h.1, ...), custom_call_target="tpu_custom_call" | custom-call | tf_op jit(solution)/shard_map/pallas_call | solution.py:685
  160.7 0.0 copy-start
  160.7 3.5 %convert.1 = f32[16,128,384]{2,1,0:T(8,128)} convert(bf16[16,128,384]{2,1,0:T(8,128)(2,1)} %bitcast.8) | non-fusion elementwise | flops 786432 | bytes 4718592 | tf_op jit(solution)/shard_map/convert_element_type | solution.py:715
  164.2 0.0 copy-done
  164.2 0.0 copy-start.1
  164.2 0.9 copy.19
  165.1 0.0 copy-done.1
  165.1 0.6 copy.20
Async XLA Ops:
  160.7 3.5 %copy-start = (bf16[16,64,384]{2,1,0:T(8,128)(2,1)S(1)}, bf16[16,64,384]{2,1,0:T(8,128)(2,1)}, u32[]{:S(2)}) copy-start(bf16[16,64,384]{2,1,0:T(8,128)(2,1)} %get-tuple-element.6) | copy-start | bytes 2359300
  164.2 0.9 copy-start.1
